TPU v7x, 32 devices: a whole 2x2x4 slice. The times are simulated.
32 devices in a mesh: region: 2 (over core), member: 16 (over z, y, x).
Axes of the slice: x: 2, y: 2, z: 4, core: 2. Of those that a mesh axis runs over, the one named last changes fastest.
Arguments:
- state: float32 [512, 16384], P('member', 'region'), may hold values from -6 to 6
- obs_pert: float32 [2, 512, 512], P('region', 'member'), may hold values from -9 to 9
- owners: int32 [2, 512], P('region'), may hold values from 0 to 15, never falling along the last dimension, each value on 1 to 128 neighbouring positions
- loc_index: int32 [2, 512], P('region'), may hold values from 0 to 7
- innov: float32 [2, 512], P('region'), may hold values from -6 to 6
- obs_var: float32 [2, 512], P('region'), may hold values from 0.5 to 2
- loc_scales: float32 [8], replicated, may hold values from 1 to 16
Outputs:
- analysis: float32 [512, 16384], P('member', 'region')
Inputs may be any that keep to these rules, and one draw needn't show every extreme that they name: Within each region the owners never fall along the batch, every patch owns at least one observation and some patch owns exactly 4 * 512 // 16.
All inputs are finite; a program needn't handle non-finite values.
Results may differ from a plain program's by a relative error of at most 0.0003.
Values sent between devices are 32-bit elements; how exact they have to be, the bound alone decides.
No kernel may reach another device: no remote copies, remote signals or barrier semaphores. Data moves between devices by JAX's collectives and lax.ppermute only.
A program may use at most 64 MiB of HBM per device.

v0:
```python
import jax
import jax.numpy as jnp
from jax import lax
from jax.experimental import pallas as pl
from jax.experimental.pallas import tpu as pltpu
from jax.sharding import PartitionSpec as P

ITERS = 6
BF16 = jnp.bfloat16
F32 = jnp.float32
NN = (((1,), (0,)), ((), ()))
NT = (((1,), (1,)), ((), ()))


def dot(a, b, dims=NN):
    return lax.dot_general(a, b, dims, preferred_element_type=F32)


def split(x):
    high = x.astype(BF16)
    return high, (x - high.astype(F32)).astype(BF16)


def dot3(a, b, dims=NN):
    return dot(a[0], b[0], dims) + dot(a[0], b[1], dims) + dot(a[1], b[0], dims)


def put(ref, x):
    ref[0], ref[1] = split(x)


def get(ref):
    return ref[0], ref[1]


def eye(order):
    shape = (order, order)
    same = lax.broadcasted_iota(jnp.int32, shape, 0) == lax.broadcasted_iota(jnp.int32, shape, 1)
    return jnp.where(same, 1.0, 0.0).astype(F32)


def row_pair(row):
    width = row.shape[1]
    high, low = split(jnp.broadcast_to(row, (8, width)))
    return jnp.concatenate([high.astype(F32), low.astype(F32)], 0).astype(BF16)


def row_dot(row, b, dims=NN):
    pair = row_pair(row)
    both = dot(pair, b[0], dims) + dot(pair, b[1], dims)
    return both[0:1] + both[8:9]


def solve_kernel(place_ref, own_ref, far_ref, info_ref, w_ref, s_ref, z_ref, q_ref, u_ref):
    order, nobs = own_ref.shape
    blocks = place_ref.shape[0] // 2
    rows = order // blocks
    ratio = info_ref[0:1] / info_ref[1:2]
    root = jnp.exp(-0.5 * ratio * ratio) * lax.rsqrt(info_ref[3:4])
    for r, ref in enumerate((own_ref, far_ref)):
        cols = slice(r * nobs, (r + 1) * nobs)
        for p in range(blocks):
            at = pl.multiple_of(place_ref[r * blocks + p] * rows, rows)
            high, low = split(ref[p * rows : (p + 1) * rows, :] * root[:, cols])
            s_ref[0, pl.ds(at, rows), cols] = high
            s_ref[1, pl.ds(at, rows), cols] = low
    s = get(s_ref)
    forcing = row_dot(root * info_ref[2:3], s, NT)
    system = dot3(s, s, NT) + (order - 1.0) * eye(order)
    inv_norm = lax.rsqrt(jnp.sum(system * system))
    first = system * inv_norm
    put(q_ref, first)
    put(z_ref, 1.5 * eye(order) - 0.5 * first)
    put(q_ref, dot3(get(q_ref), get(z_ref)))

    def sweep(i, carry):
        put(u_ref, 1.5 * eye(order) - 0.5 * dot3(get(z_ref), get(q_ref)))
        next_q = dot3(get(q_ref), get(u_ref))
        next_z = dot3(get(u_ref), get(z_ref))
        put(q_ref, next_q)
        put(z_ref, next_z)
        return carry

    lax.fori_loop(0, ITERS - 2, sweep, 0)
    put(u_ref, 1.5 * eye(order) - 0.5 * dot3(get(z_ref), get(q_ref)))
    z = dot3(get(u_ref), get(z_ref))
    put(z_ref, z)
    shift = row_dot(row_dot(forcing, get(z_ref)), get(z_ref)) * inv_norm
    put(w_ref, (jnp.sqrt(order - 1.0) * jnp.sqrt(inv_norm)) * z + shift)


def solve(place, own, far, info):
    order, nobs = own.shape
    vmem = pl.BlockSpec(memory_space=pltpu.VMEM)
    return pl.pallas_call(
        solve_kernel,
        out_shape=jax.ShapeDtypeStruct((2, order, order), BF16),
        in_specs=[pl.BlockSpec(memory_space=pltpu.SMEM), vmem, vmem, vmem],
        out_specs=vmem,
        scratch_shapes=[pltpu.VMEM((2, order, 2 * nobs), BF16)]
        + [pltpu.VMEM((2, order, order), BF16)] * 3,
        compiler_params=pltpu.CompilerParams(vmem_limit_bytes=40 << 20),
        cost_estimate=pl.CostEstimate(
            flops=18 * 3 * 2 * order**3, bytes_accessed=8 * order * nobs, transcendentals=0
        ),
    )(place, own, far, info)


def update_kernel(w_ref, x_ref, o_ref):
    x = x_ref[...]
    center = jnp.mean(x, axis=0, keepdims=True)
    o_ref[...] = center + dot3(get(w_ref), split(x - center))


def update(weights, members):
    vmem = pl.BlockSpec(memory_space=pltpu.VMEM)
    order, cells = members.shape
    return pl.pallas_call(
        update_kernel,
        out_shape=jax.ShapeDtypeStruct(members.shape, F32),
        in_specs=[vmem, vmem],
        out_specs=vmem,
        compiler_params=pltpu.CompilerParams(vmem_limit_bytes=24 << 20),
        cost_estimate=pl.CostEstimate(
            flops=3 * 2 * order * order * cells, bytes_accessed=12 * order * cells, transcendentals=0
        ),
    )(weights, members)


def swap_by(block, count, first, second):
    route = [(i, i ^ first) for i in range(count)]
    route += [(count + i, count + (i ^ second)) for i in range(count)]
    return lax.ppermute(block, ("region", "member"), route)


def gather_rows(shard, count, region):
    low = 1 << (count.bit_length() - 1) // 2
    if low * low != count or shard.shape[0] % 16:
        whole = lax.all_gather(shard, "member", axis=0, tiled=True)
        blocks = whole.shape[0] // 32
        return whole, jnp.arange(2 * blocks, dtype=jnp.int32) % blocks
    far_steps = [step * low for step in range(low)][::-1][:-1]
    near_steps = list(range(low))[::-1][:-1]
    held = shard
    for one, two in ((far_steps, near_steps), (near_steps, far_steps)):
        held = jnp.concatenate([held] + [swap_by(held, count, a, b) for a, b in zip(one, two)])
    far_off, near_off = jnp.array([0] + far_steps), jnp.array([0] + near_steps)
    far_first = (near_off[:, None] ^ far_off[None, :]).reshape(-1)
    near_first = (far_off[:, None] ^ near_off[None, :]).reshape(-1)
    own = jnp.where(region == 0, far_first, near_first)
    other = jnp.where(region == 0, near_first, far_first)
    place = lax.axis_index("member") ^ jnp.concatenate([own, other])
    return held, place.astype(jnp.int32)


def local(state, obs_pert, owners, loc_index, innov, obs_var, loc_scales):
    region = lax.axis_index("region")
    patch_id = lax.axis_index("member")
    npatch = lax.axis_size("member")
    cycle_len = float(lax.axis_size("region") * npatch)
    table = jnp.arange(loc_scales.shape[0], dtype=jnp.int32)
    choose = (loc_index[0][:, None] == table).astype(F32)
    scales = jnp.sum(choose * loc_scales, axis=1)
    positions = (region * npatch + owners[0]).astype(F32)
    obs_info = jnp.stack([positions, scales, innov[0], obs_var[0]])
    regions = [(0, 1), (1, 0)]
    far_info = lax.ppermute(obs_info, "region", regions)
    own_pert, place = gather_rows(obs_pert[0], npatch, region)
    far_pert = lax.ppermute(own_pert, "region", regions)
    info_all = jnp.concatenate([obs_info, far_info], axis=1)
    distance = jnp.abs((region * npatch + patch_id).astype(F32) - info_all[0])
    distance = jnp.minimum(distance, cycle_len - distance)
    info_all = jnp.concatenate([distance[None], info_all[1:]])
    weights = solve(place, own_pert, far_pert, info_all)
    members = lax.all_to_all(state, "member", split_axis=1, concat_axis=0, tiled=True)
    updated = update(weights, members)
    return lax.all_to_all(updated, "member", split_axis=0, concat_axis=1, tiled=True)


def solution(mesh):
    placed = (
        P("member", "region"),
        P("region", "member", None),
        P("region", None),
        P("region", None),
        P("region", None),
        P("region", None),
        P(),
    )
    return jax.shard_map(
        local, mesh=mesh, in_specs=placed, out_specs=P("member", "region"), check_vma=False
    )
```

profile of v0, /device:TPU:0, one launch (start us, length us, event | category | flops | bytes accessed | tf_op | source)
XLA Modules:
  0.0 87.2 jit_solution(9339413482438961292)
XLA Ops:
  0.0 0.0 copy-start.3
  0.0 5.0 %collective-permute-start = (f32[32,512]{1,0:T(8,128)}, f32[32,512]{1,0:T(8,128)S(1)}, u32[]{:S(2)}, u32[]{:S(2)}) collective-permute-start(f32[32,512]{1,0:T(8,128)} %bitcast.20), channel_id=1, source_target_pairs={{0,12},{1,13},{2,14},{3,15},{4,8},{5,9},{6,10},{7,11},{8,4},{9,5},... | collective-permute-start | bytes 196616 | tf_op jit(solution)/shard_map/ppermute | solution.py:133
  5.1 0.0 collective-permute-start.1
  5.1 0.6 collective-permute-start.2
  5.7 0.9 %constant_dynamic-update-slice_fusion.6 = f32[512,512]{1,0:T(8,128)S(1)} fusion(f32[1,32,512]{2,1,0:T(8,128)} %param.10), kind=kLoop, calls=%fused_computation.14 | loop fusion | bytes 131072
  6.6 1.1 %collective-permute-done = f32[32,512]{1,0:T(8,128)S(1)} collective-permute-done((f32[32,512]{1,0:T(8,128)}, f32[32,512]{1,0:T(8,128)S(1)}, u32[]{:S(2)}, u32[]{:S(2)}) %collective-permute-start) | collective-permute-done | bytes 65568 | tf_op jit(solution)/shard_map/ppermute | solution.py:133
  7.6 2.8 %collective-permute-done.1 = f32[32,512]{1,0:T(8,128)S(1)} collective-permute-done((f32[32,512]{1,0:T(8,128)}, f32[32,512]{1,0:T(8,128)S(1)}, u32[]{:S(2)}, u32[]{:S(2)}) %collective-permute-start.1) | collective-permute-done | bytes 65568 | tf_op jit(solution)/shard_map/ppermute | solution.py:133
  10.4 0.0 collective-permute-done.2
  10.4 0.0 copy-done.3
  10.5 0.0 copy-start.2
  10.5 4.2 %collective-permute-start.3 = (f32[128,512]{1,0:T(8,128)S(1)}, f32[128,512]{1,0:T(8,128)S(1)}, u32[]{:S(2)}, u32[]{:S(2)}) collective-permute-start(f32[128,512]{1,0:T(8,128)S(1)} %pad_maximum_fusion), channel_id=1, source_target_pairs={{0,3},{1,2},{2,1},{3,0},{4,7},{5,6},{6,5},{7,4},{8,11},{9,10},{10,... | collective-permute-start | bytes 786440 | tf_op jit(solution)/shard_map/ppermute | solution.py:133
  14.6 0.0 collective-permute-start.4
  14.6 0.6 collective-permute-start.5
  15.3 3.8 %collective-permute-done.3 = f32[128,512]{1,0:T(8,128)S(1)} collective-permute-done((f32[128,512]{1,0:T(8,128)S(1)}, f32[128,512]{1,0:T(8,128)S(1)}, u32[]{:S(2)}, u32[]{:S(2)}) %collective-permute-start.3) | collective-permute-done | bytes 262176 | tf_op jit(solution)/shard_map/ppermute | solution.py:133
  19.1 2.7 %collective-permute-done.4 = f32[128,512]{1,0:T(8,128)S(1)} collective-permute-done((f32[128,512]{1,0:T(8,128)S(1)}, f32[128,512]{1,0:T(8,128)S(1)}, u32[]{:S(2)}, u32[]{:S(2)}) %collective-permute-start.4) | collective-permute-done | bytes 262176 | tf_op jit(solution)/shard_map/ppermute | solution.py:133
  21.8 0.0 collective-permute-done.5
  21.9 0.1 collective-permute-start.6
  21.9 0.0 copy-done.2
  22.0 1.1 %copy.17 = f32[4,16,8,512]{3,2,0,1:T(8,128)} copy(f32[4,16,8,512]{3,2,1,0:T(8,128)S(1)} %bitcast.19) | data formatting | bytes 2097152 | tf_op jit(solution)/shard_map/all_to_all | solution.py:175
  23.0 0.0 copy-start.4
  23.0 0.0 copy-start.5
  23.0 4.9 %all-to-all-start = ((f32[32,16,512]{2,0,1:T(8,128)}), f32[32,16,512]{2,0,1:T(8,128)S(1)}, u32[]{:S(2)}, u32[]{:S(2)}) async-start(f32[32,16,512]{2,0,1:T(8,128)} %bitcast.17), calls=%async_computation | async-start | bytes 2097152 | tf_op jit(solution)/shard_map/all_to_all | solution.py:175
  27.9 0.0 copy-start.6
  27.9 0.0 copy-start.10
  28.0 0.7 copy-done.6
  28.6 0.0 copy-done.10
  28.6 0.0 copy-start.7
  28.6 0.1 select_reduce_fusion
  28.7 0.6 copy-done.7
  29.3 0.0 copy-done.4
  29.3 0.0 copy-done.5
  29.3 0.1 collective-permute-start.7
  29.4 0.0 copy-start.8
  29.4 0.0 copy-start.9
  29.4 0.6 copy-done.8
  30.1 0.0 copy-done.9
  30.1 0.1 xor_select_fusion.1
  30.2 0.1 select_n.20
  30.3 0.1 select_n.22
  30.3 0.1 add_xor_fusion.place_ref
  30.4 0.2 collective-permute-done.7
  30.6 0.0 collective-permute-done.6.far_ref
  30.6 0.0 copy-start
  30.6 1.0 %copy-done = f32[512,512]{1,0:T(8,128)} copy-done((f32[512,512]{1,0:T(8,128)}, f32[512,512]{1,0:T(8,128)S(1)}, u32[]{:S(2)}) %copy-start) | copy-done | bytes 1048600
  31.6 0.0 copy-start.1
  31.6 1.2 %copy-done.1 = f32[512,512]{1,0:T(8,128)S(1)} copy-done((f32[512,512]{1,0:T(8,128)S(1)}, f32[512,512]{1,0:T(8,128)}, u32[]{:S(2)}) %copy-start.1) | copy-done | bytes 1048600
  32.8 18.8 %shard_map.91.w_ref = bf16[2,512,512]{2,1,0:T(8,128)(2,1)S(1)} custom-call(s32[32]{0:T(128)S(1)} %add_xor_fusion.place_ref, f32[512,512]{1,0:T(8,128)S(1)} %constant_dynamic-update-slice_fusion.own_ref, f32[512,512]{1,0:T(8,128)S(1)} %copy-done.1, f32[4,1024]{1,0:T(4,128)S(1)} %fusion.info_ref), custom_call_target="tpu_custom_call" | custom-call | flops 14495514624 | bytes 2097152 | tf_op jit(solution)/shard_map/pallas_call | solution.py:95
  51.6 0.9 %all-to-all-done = f32[32,16,512]{2,0,1:T(8,128)S(1)} async-done(((f32[32,16,512]{2,0,1:T(8,128)}), f32[32,16,512]{2,0,1:T(8,128)S(1)}, u32[]{:S(2)}, u32[]{:S(2)}) %all-to-all-start) | async-done | bytes 1048608 | tf_op jit(solution)/shard_map/all_to_all | solution.py:175
  52.5 1.1 %shard_map.92 = f32[512,512]{1,0:T(8,128)S(1)} custom-call(bf16[2,512,512]{2,1,0:T(8,128)(2,1)S(1)} %shard_map.91.w_ref, f32[512,512]{1,0:T(8,128)S(1)} %bitcast.15), custom_call_target="tpu_custom_call" | custom-call | flops 805306368 | bytes 3145728 | tf_op jit(solution)/shard_map/pallas_call | solution.py:118
  53.6 32.5 %all_to_all.38 = f32[16,32,512]{2,1,0:T(8,128)S(1)} all-to-all(f32[16,32,512]{2,1,0:T(8,128)S(1)} %bitcast.16), channel_id=1, replica_groups=mesh['region'=2,'member'=16] {'member'}, dimensions={0} | all-to-all | bytes 2097152 | tf_op jit(solution)/shard_map/all_to_all | solution.py:177
  86.2 1.1 %copy.15 = f32[16,4,8,512]{3,2,0,1:T(8,128)} copy(f32[16,4,8,512]{3,2,1,0:T(8,128)S(1)} %bitcast.18) | data formatting | bytes 2097152 | tf_op jit(solution)/shard_map/all_to_all | solution.py:177
  (11 shorter events, 0.1 us)
Async XLA Ops:
  0.0 10.4 %copy-start.3 = (f32[1,32,512]{2,1,0:T(8,128)S(1)}, f32[1,32,512]{2,1,0:T(8,128)}, u32[]{:S(2)}) copy-start(f32[1,32,512]{2,1,0:T(8,128)} %param.10) | copy-start | bytes 196612
  0.0 7.6 %collective-permute-start = (f32[32,512]{1,0:T(8,128)}, f32[32,512]{1,0:T(8,128)S(1)}, u32[]{:S(2)}, u32[]{:S(2)}) collective-permute-start(f32[32,512]{1,0:T(8,128)} %bitcast.20), channel_id=1, source_target_pairs={{0,12},{1,13},{2,14},{3,15},{4,8},{5,9},{6,10},{7,11},{8,4},{9,5},... | collective-permute-start | bytes 196616 | tf_op jit(solution)/shard_map/ppermute | solution.py:133
  5.1 5.4 %collective-permute-start.1 = (f32[32,512]{1,0:T(8,128)}, f32[32,512]{1,0:T(8,128)S(1)}, u32[]{:S(2)}, u32[]{:S(2)}) collective-permute-start(f32[32,512]{1,0:T(8,128)} %bitcast.21), channel_id=1, source_target_pairs={{0,8},{1,9},{2,10},{3,11},{4,12},{5,13},{6,14},{7,15},{8,0},{9,1},... | collective-permute-start | bytes 196616 | tf_op jit(solution)/shard_map/ppermute | solution.py:133
  5.1 5.4 %collective-permute-start.2 = (f32[32,512]{1,0:T(8,128)}, f32[32,512]{1,0:T(8,128)S(1)}, u32[]{:S(2)}, u32[]{:S(2)}) collective-permute-start(f32[32,512]{1,0:T(8,128)} %bitcast.22), channel_id=1, source_target_pairs={{0,4},{1,5},{2,6},{3,7},{4,0},{5,1},{6,2},{7,3},{8,12},{9,13},{10,... | collective-permute-start | bytes 196616 | tf_op jit(solution)/shard_map/ppermute | solution.py:133
  10.5 11.5 %copy-start.2 = (f32[32,8192]{1,0:T(8,128)S(1)}, f32[32,8192]{1,0:T(8,128)}, u32[]{:S(2)}) copy-start(f32[32,8192]{1,0:T(8,128)} %param.9) | copy-start | bytes 3145732
  10.5 8.6 %collective-permute-start.3 = (f32[128,512]{1,0:T(8,128)S(1)}, f32[128,512]{1,0:T(8,128)S(1)}, u32[]{:S(2)}, u32[]{:S(2)}) collective-permute-start(f32[128,512]{1,0:T(8,128)S(1)} %pad_maximum_fusion), channel_id=1, source_target_pairs={{0,3},{1,2},{2,1},{3,0},{4,7},{5,6},{6,5},{7,4},{8,11},{9,10},{10,... | collective-permute-start | bytes 786440 | tf_op jit(solution)/shard_map/ppermute | solution.py:133
  14.6 7.2 %collective-permute-start.4 = (f32[128,512]{1,0:T(8,128)S(1)}, f32[128,512]{1,0:T(8,128)S(1)}, u32[]{:S(2)}, u32[]{:S(2)}) collective-permute-start(f32[128,512]{1,0:T(8,128)S(1)} %pad_maximum_fusion), channel_id=1, source_target_pairs={{0,2},{1,3},{2,0},{3,1},{4,6},{5,7},{6,4},{7,5},{8,10},{9,11},{10,... | collective-permute-start | bytes 786440 | tf_op jit(solution)/shard_map/ppermute | solution.py:133
  14.6 7.2 %collective-permute-start.5 = (f32[128,512]{1,0:T(8,128)S(1)}, f32[128,512]{1,0:T(8,128)S(1)}, u32[]{:S(2)}, u32[]{:S(2)}) collective-permute-start(f32[128,512]{1,0:T(8,128)S(1)} %pad_maximum_fusion), channel_id=1, source_target_pairs={{0,1},{1,0},{2,3},{3,2},{4,5},{5,4},{6,7},{7,6},{8,9},{9,8},{10,11... | collective-permute-start | bytes 786440 | tf_op jit(solution)/shard_map/ppermute | solution.py:133
  21.9 8.8 %collective-permute-start.6 = (f32[512,512]{1,0:T(8,128)S(1)}, f32[512,512]{1,0:T(8,128)S(1)}, u32[]{:S(2)}, u32[]{:S(2)}) collective-permute-start(f32[512,512]{1,0:T(8,128)S(1)} %constant_dynamic-update-slice_fusion.own_ref), channel_id=1, source_target_pairs={{0,16},{16,0},{1,17},{17,1},{2,18},{18,2},{3,19},{19,3},{4,20},{20... | collective-permute-start | bytes 3145736 | tf_op jit(solution)/shard_map/ppermute | solution.py:169
  23.0 6.3 %copy-start.4 = (f32[1,512]{1,0:T(1,128)S(1)}, f32[1,512]{1,0:T(1,128)}, u32[]{:S(2)}) copy-start(f32[1,512]{1,0:T(1,128)} %param.14) | copy-start | bytes 6148
  23.0 6.3 %copy-start.5 = (f32[1,512]{1,0:T(1,128)S(1)}, f32[1,512]{1,0:T(1,128)}, u32[]{:S(2)}) copy-start(f32[1,512]{1,0:T(1,128)} %param.13) | copy-start | bytes 6148
  23.0 29.5 %all-to-all-start = ((f32[32,16,512]{2,0,1:T(8,128)}), f32[32,16,512]{2,0,1:T(8,128)S(1)}, u32[]{:S(2)}, u32[]{:S(2)}) async-start(f32[32,16,512]{2,0,1:T(8,128)} %bitcast.17), calls=%async_computation | async-start | bytes 2097152 | tf_op jit(solution)/shard_map/all_to_all | solution.py:175
  27.9 0.7 copy-start.6
  27.9 0.7 copy-start.10
  28.6 0.7 copy-start.7
  29.3 1.2 %collective-permute-start.7 = (f32[4,512]{1,0:T(4,128)S(1)}, f32[4,512]{1,0:T(4,128)S(1)}, u32[]{:S(2)}, u32[]{:S(2)}) collective-permute-start(f32[4,512]{1,0:T(4,128)S(1)} %pad_maximum_fusion.1), channel_id=1, source_target_pairs={{0,16},{16,0},{1,17},{17,1},{2,18},{18,2},{3,19},{19,3},{4,20},{20... | collective-permute-start | bytes 24584 | tf_op jit(solution)/shard_map/ppermute | solution.py:167
  29.4 0.7 copy-start.8
  29.4 0.7 copy-start.9
  30.6 1.0 %copy-start = (f32[512,512]{1,0:T(8,128)}, f32[512,512]{1,0:T(8,128)S(1)}, u32[]{:S(2)}) copy-start(f32[512,512]{1,0:T(8,128)S(1)} %collective-permute-done.6.far_ref) | copy-start | bytes 3145732
  31.6 1.2 %copy-start.1 = (f32[512,512]{1,0:T(8,128)S(1)}, f32[512,512]{1,0:T(8,128)}, u32[]{:S(2)}) copy-start(f32[512,512]{1,0:T(8,128)} %copy-done) | copy-start | bytes 3145732
where the time goes:
time: 87.6 us; the launch traced here: 87.2 us
  blocking collectives  32.5 us (37%)
  Pallas kernels  19.9 us (23%)
  starting transfers between devices  15.5 us (18%)
  waiting for transfers between devices  11.4 us (13%)
  local copies, waits for them, and re-layouts  7.38 us (8%)
    all_to_all x1, blocking collectives, local(): lax.all_to_all(updated, 'member', split_axis=0, concat_axis=1, tiled=True)  32.5 us
    pallas_call x1, Pallas kernels, solve(): pl.pallas_call(solve_kernel, out_shape=jax.ShapeDtypeStruct((2, order, or...  18.8 us
    ppermute x6, starting transfers between devices, swap_by(): return lax.ppermute(block, ('region', 'member'), route)  10.5 us
    ppermute x6, waiting for transfers between devices, swap_by(): return lax.ppermute(block, ('region', 'member'), route)  10.3 us
    unnamed x28, local copies, waits for them, and re-layouts  5.06 us
    all_to_all x1, starting transfers between devices, local(): lax.all_to_all(state, 'member', split_axis=1, concat_axis=0, tiled=True)  4.89 us
  transfers between devices with their start and end apart: 9, of which 6 were waited for; matrix products, arithmetic and copies ran while one was open for 3% of the time, Pallas kernels for 22%

commit v1 on v0

--- a/solution.py
+++ b/solution.py
@@ -1,3 +1,5 @@
+import functools
+
 import jax
 import jax.numpy as jnp
 from jax import lax
@@ -51,21 +53,59 @@
     return both[0:1] + both[8:9]
 
 
-def solve_kernel(place_ref, own_ref, far_ref, info_ref, w_ref, s_ref, z_ref, q_ref, u_ref):
-    order, nobs = own_ref.shape
-    blocks = place_ref.shape[0] // 2
+def pack_kernel(owner_ref, index_ref, innov_ref, var_ref, table_ref, o_ref):
+    first = lax.axis_index("region") * lax.axis_size("member")
+    index = index_ref[...]
+    scale = jnp.zeros(index.shape, F32)
+    for entry in range(table_ref.shape[0]):
+        scale = jnp.where(index == entry, table_ref[entry], scale)
+    o_ref[...] = jnp.zeros(o_ref.shape, F32)
+    o_ref[0:1] = (owner_ref[...] + first).astype(F32)
+    o_ref[1:2] = scale
+    o_ref[2:3] = innov_ref[...]
+    o_ref[3:4] = var_ref[...]
+
+
+def pack(owners, loc_index, innov, obs_var, loc_scales):
+    vmem = pl.BlockSpec(memory_space=pltpu.VMEM)
+    return pl.pallas_call(
+        pack_kernel,
+        out_shape=jax.ShapeDtypeStruct((8, owners.shape[1]), F32),
+        in_specs=[vmem] * 4 + [pl.BlockSpec(memory_space=pltpu.SMEM)],
+        out_specs=vmem,
+    )(owners, loc_index, innov, obs_var, loc_scales)
+
+
+def solve_kernel(orders, count, *refs):
+    nparts = (count - 2) // 2
+    own_refs, far_refs = refs[:nparts], refs[nparts : 2 * nparts]
+    own_info, far_info, w_ref, s_ref, z_ref, q_ref, u_ref = refs[2 * nparts :]
+    order = w_ref.shape[1]
+    nobs = own_info.shape[1]
+    blocks = len(orders[0])
     rows = order // blocks
-    ratio = info_ref[0:1] / info_ref[1:2]
-    root = jnp.exp(-0.5 * ratio * ratio) * lax.rsqrt(info_ref[3:4])
-    for r, ref in enumerate((own_ref, far_ref)):
+    region, member = lax.axis_index("region"), lax.axis_index("member")
+    nmember = lax.axis_size("member")
+    patch = (region * nmember + member).astype(F32)
+    cycle = float(nmember * lax.axis_size("region"))
+    info = jnp.concatenate([own_info[...], far_info[...]], axis=1)
+    dist = jnp.abs(patch - info[0:1])
+    ratio = jnp.minimum(dist, cycle - dist) / info[1:2]
+    root = jnp.exp(-0.5 * ratio * ratio) * lax.rsqrt(info[3:4])
+    for r, parts in enumerate((own_refs, far_refs)):
         cols = slice(r * nobs, (r + 1) * nobs)
+        per_part = blocks // nparts
         for p in range(blocks):
-            at = pl.multiple_of(place_ref[r * blocks + p] * rows, rows)
-            high, low = split(ref[p * rows : (p + 1) * rows, :] * root[:, cols])
+            offset = jnp.where(region == r, orders[0][p], orders[1][p])
+            block = member ^ offset if nparts > 1 else offset
+            at = pl.multiple_of(block * rows, rows)
+            place = p % per_part * rows
+            data = parts[p // per_part][place : place + rows, :]
+            high, low = split(data * root[:, cols])
             s_ref[0, pl.ds(at, rows), cols] = high
             s_ref[1, pl.ds(at, rows), cols] = low
     s = get(s_ref)
-    forcing = row_dot(root * info_ref[2:3], s, NT)
+    forcing = row_dot(root * info[2:3], s, NT)
     system = dot3(s, s, NT) + (order - 1.0) * eye(order)
     inv_norm = lax.rsqrt(jnp.sum(system * system))
     first = system * inv_norm
@@ -89,21 +129,23 @@
     put(w_ref, (jnp.sqrt(order - 1.0) * jnp.sqrt(inv_norm)) * z + shift)
 
 
-def solve(place, own, far, info):
-    order, nobs = own.shape
+def solve(orders, own_parts, far_parts, own_info, far_info):
+    order = sum(part.shape[0] for part in own_parts)
+    nobs = own_parts[0].shape[1]
     vmem = pl.BlockSpec(memory_space=pltpu.VMEM)
+    operands = [*own_parts, *far_parts, own_info, far_info]
     return pl.pallas_call(
-        solve_kernel,
+        functools.partial(solve_kernel, orders, len(operands)),
         out_shape=jax.ShapeDtypeStruct((2, order, order), BF16),
-        in_specs=[pl.BlockSpec(memory_space=pltpu.SMEM), vmem, vmem, vmem],
+        in_specs=[vmem] * len(operands),
         out_specs=vmem,
         scratch_shapes=[pltpu.VMEM((2, order, 2 * nobs), BF16)]
         + [pltpu.VMEM((2, order, order), BF16)] * 3,
         compiler_params=pltpu.CompilerParams(vmem_limit_bytes=40 << 20),
         cost_estimate=pl.CostEstimate(
-            flops=18 * 3 * 2 * order**3, bytes_accessed=8 * order * nobs, transcendentals=0
+            flops=20 * 3 * 2 * order**3, bytes_accessed=8 * order * nobs, transcendentals=0
         ),
-    )(place, own, far, info)
+    )(*operands)
 
 
 def update_kernel(w_ref, x_ref, o_ref):
@@ -133,45 +175,37 @@
     return lax.ppermute(block, ("region", "member"), route)
 
 
-def gather_rows(shard, count, region):
+REGIONS = [(0, 1), (1, 0)]
+
+
+def from_region(block):
+    return lax.ppermute(block, "region", REGIONS)
+
+
+def gather_rows(shard, info, count):
     low = 1 << (count.bit_length() - 1) // 2
     if low * low != count or shard.shape[0] % 16:
         whole = lax.all_gather(shard, "member", axis=0, tiled=True)
-        blocks = whole.shape[0] // 32
-        return whole, jnp.arange(2 * blocks, dtype=jnp.int32) % blocks
+        same = list(range(whole.shape[0] // 32))
+        return (same, same), [whole], [from_region(whole)], from_region(info)
     far_steps = [step * low for step in range(low)][::-1][:-1]
     near_steps = list(range(low))[::-1][:-1]
-    held = shard
-    for one, two in ((far_steps, near_steps), (near_steps, far_steps)):
-        held = jnp.concatenate([held] + [swap_by(held, count, a, b) for a, b in zip(one, two)])
-    far_off, near_off = jnp.array([0] + far_steps), jnp.array([0] + near_steps)
-    far_first = (near_off[:, None] ^ far_off[None, :]).reshape(-1)
-    near_first = (far_off[:, None] ^ near_off[None, :]).reshape(-1)
-    own = jnp.where(region == 0, far_first, near_first)
-    other = jnp.where(region == 0, near_first, far_first)
-    place = lax.axis_index("member") ^ jnp.concatenate([own, other])
-    return held, place.astype(jnp.int32)
+    got = [swap_by(shard, count, a, b) for a, b in zip(far_steps, near_steps)]
+    held = jnp.concatenate([shard] + got)
+    far_info = from_region(info)
+    held, far_info = lax.optimization_barrier((held, far_info))
+    own = [held] + [swap_by(held, count, a, b) for a, b in zip(near_steps, far_steps)]
+    far = [from_region(part) for part in own]
+    far_first = [n ^ f for n in [0] + near_steps for f in [0] + far_steps]
+    near_first = [f ^ n for f in [0] + far_steps for n in [0] + near_steps]
+    return (far_first, near_first), own, far, far_info
 
 
 def local(state, obs_pert, owners, loc_index, innov, obs_var, loc_scales):
-    region = lax.axis_index("region")
-    patch_id = lax.axis_index("member")
     npatch = lax.axis_size("member")
-    cycle_len = float(lax.axis_size("region") * npatch)
-    table = jnp.arange(loc_scales.shape[0], dtype=jnp.int32)
-    choose = (loc_index[0][:, None] == table).astype(F32)
-    scales = jnp.sum(choose * loc_scales, axis=1)
-    positions = (region * npatch + owners[0]).astype(F32)
-    obs_info = jnp.stack([positions, scales, innov[0], obs_var[0]])
-    regions = [(0, 1), (1, 0)]
-    far_info = lax.ppermute(obs_info, "region", regions)
-    own_pert, place = gather_rows(obs_pert[0], npatch, region)
-    far_pert = lax.ppermute(own_pert, "region", regions)
-    info_all = jnp.concatenate([obs_info, far_info], axis=1)
-    distance = jnp.abs((region * npatch + patch_id).astype(F32) - info_all[0])
-    distance = jnp.minimum(distance, cycle_len - distance)
-    info_all = jnp.concatenate([distance[None], info_all[1:]])
-    weights = solve(place, own_pert, far_pert, info_all)
+    info = pack(owners, loc_index, innov, obs_var, loc_scales)
+    orders, own, far, far_info = gather_rows(obs_pert[0], info, npatch)
+    weights = solve(orders, own, far, info, far_info)
     members = lax.all_to_all(state, "member", split_axis=1, concat_axis=0, tiled=True)
     updated = update(weights, members)
     return lax.all_to_all(updated, "member", split_axis=0, concat_axis=1, tiled=True)

time: 87.6 us -> 82.3 us (0.939)
  local copies, waits for them, and re-layouts: 7.38 us -> 3.35 us
  waiting for transfers between devices: 11.4 us -> 8.97 us
  starting transfers between devices: 15.5 us -> 14.4 us
  Pallas kernels: 19.9 us -> 20.8 us
  blocking collectives: 32.5 us -> 33.4 us
    ppermute x6, waiting for transfers between devices: 10.3 us -> 5.01 us  [swap_by(): return lax.ppermute(block, ('region', 'member'), route)]
    unnamed x28 -> x2, local copies, waits for them, and re-layouts: 5.06 us -> 0.01 us
    all_to_all x1, waiting for transfers between devices: 0.89 us -> 2.48 us  [local(): lax.all_to_all(state, 'member', split_axis=1, concat_axis=0, tiled=True)]
    ppermute x6, starting transfers between devices: 10.5 us -> 9.17 us  [swap_by(): return lax.ppermute(block, ('region', 'member'), route)]
    ppermute x2 -> x5, waiting for transfers between devices: 0.17 us -> 1.48 us  [from_region(): return lax.ppermute(block, 'region', REGIONS)]
    all_to_all x1, local copies, waits for them, and re-layouts: 1.07 us -> 2.29 us  [local(): lax.all_to_all(state, 'member', split_axis=1, concat_axis=0, tiled=True)]
    ppermute x2 -> x5, starting transfers between devices: 0.14 us -> 1.07 us  [from_region(): return lax.ppermute(block, 'region', REGIONS)]
    all_to_all x1, blocking collectives: 32.5 us -> 33.4 us  [local(): lax.all_to_all(updated, 'member', split_axis=0, concat_axis=1, tiled=True)]
  transfers between devices with their start and end apart: 9 -> 12, of which waited for: 6 -> 8; matrix products, arithmetic and copies ran while one was open for 3% -> 4% of each run, Pallas kernels for 22% -> 24%
where the time goes in v1:
time: 82.3 us; the launch traced here: 81.9 us
  blocking collectives  33.4 us (41%)
  Pallas kernels  20.8 us (25%)
  starting transfers between devices  14.4 us (17%)
  waiting for transfers between devices  8.97 us (11%)
  local copies, waits for them, and re-layouts  3.35 us (4%)
  other arithmetic  0.86 us (1%)
    all_to_all x1, blocking collectives, local(): lax.all_to_all(updated, 'member', split_axis=0, concat_axis=1, tiled=True)  33.4 us
    pallas_call x1, Pallas kernels, solve(): pl.pallas_call(functools.partial(solve_kernel, orders, len(operands)), ou...  18.2 us
    ppermute x6, starting transfers between devices, swap_by(): return lax.ppermute(block, ('region', 'member'), route)  9.17 us
    ppermute x6, waiting for transfers between devices, swap_by(): return lax.ppermute(block, ('region', 'member'), route)  5.01 us
    all_to_all x1, starting transfers between devices, local(): lax.all_to_all(state, 'member', split_axis=1, concat_axis=0, tiled=True)  4.2 us
    all_to_all x1, waiting for transfers between devices, local(): lax.all_to_all(state, 'member', split_axis=1, concat_axis=0, tiled=True)  2.48 us
    all_to_all x1, local copies, waits for them, and re-layouts, local(): lax.all_to_all(state, 'member', split_axis=1, concat_axis=0, tiled=True)  2.29 us
  transfers between devices with their start and end apart: 12, of which 8 were waited for; matrix products, arithmetic and copies ran while one was open for 4% of the time, Pallas kernels for 24%

profile of v1, /device:TPU:0, one launch (start us, length us, event | category | flops | bytes accessed | tf_op | source)
XLA Modules:
  0.0 81.9 jit_solution(17389950980403764576)
XLA Ops:
  0.0 3.0 %collective-permute-start.2 = (f32[32,512]{1,0:T(8,128)}, f32[32,512]{1,0:T(8,128)S(1)}, u32[]{:S(2)}, u32[]{:S(2)}) collective-permute-start(f32[32,512]{1,0:T(8,128)} %bitcast.16), channel_id=1, source_target_pairs={{0,4},{1,5},{2,6},{3,7},{4,0},{5,1},{6,2},{7,3},{8,12},{9,13},{10,... | collective-permute-start | bytes 196616 | tf_op jit(solution)/shard_map/ppermute | solution.py:175
  3.0 2.6 %collective-permute-start.1 = (f32[32,512]{1,0:T(8,128)}, f32[32,512]{1,0:T(8,128)S(1)}, u32[]{:S(2)}, u32[]{:S(2)}) collective-permute-start(f32[32,512]{1,0:T(8,128)} %bitcast.17), channel_id=1, source_target_pairs={{0,8},{1,9},{2,10},{3,11},{4,12},{5,13},{6,14},{7,15},{8,0},{9,1},... | collective-permute-start | bytes 196616 | tf_op jit(solution)/shard_map/ppermute | solution.py:175
  5.6 0.0 collective-permute-start
  5.6 1.4 %shard_map.73.refs_8_ = f32[8,512]{1,0:T(8,128)} custom-call(s32[1,512]{1,0:T(1,128)} %owner_ref.1, s32[1,512]{1,0:T(1,128)} %index_ref.1, f32[1,512]{1,0:T(1,128)} %innov_ref.1, f32[1,512]{1,0:T(1,128)} %var_ref.1, f32[8]{0:T(128)} %table_ref.1), custom_call_target="tpu_custom_call" | custom-call | tf_op jit(solution)/shard_map/pallas_call | solution.py:71
  7.0 0.0 collective-permute-start.3
  7.0 0.0 collective-permute-done.2
  7.0 2.1 %collective-permute-done.1 = f32[32,512]{1,0:T(8,128)S(1)} collective-permute-done((f32[32,512]{1,0:T(8,128)}, f32[32,512]{1,0:T(8,128)S(1)}, u32[]{:S(2)}, u32[]{:S(2)}) %collective-permute-start.1) | collective-permute-done | bytes 65568 | tf_op jit(solution)/shard_map/ppermute | solution.py:175
  9.1 2.8 %collective-permute-done = f32[32,512]{1,0:T(8,128)S(1)} collective-permute-done((f32[32,512]{1,0:T(8,128)}, f32[32,512]{1,0:T(8,128)S(1)}, u32[]{:S(2)}, u32[]{:S(2)}) %collective-permute-start) | collective-permute-done | bytes 65568 | tf_op jit(solution)/shard_map/ppermute | solution.py:175
  11.9 0.9 %pad_maximum_fusion.refs_0_ = f32[128,512]{1,0:T(8,128)S(1)} fusion(f32[32,512]{1,0:T(8,128)S(1)} %collective-permute-done.2, f32[32,512]{1,0:T(8,128)S(1)} %collective-permute-done.1, f32[32,512]{1,0:T(8,128)S(1)} %collective-permute-done, f32[32,512]{1,0:T(8,128)} %bitcast.19), kind=kLoop, calls=%fused_computation.1 | loop fusion | flops 196608 | bytes 524288 | tf_op jit(solution)/shard_map/concatenate | solution.py:194
  12.8 0.0 collective-permute-done.3.refs_9_
  12.8 1.6 %collective-permute-start.6 = (f32[128,512]{1,0:T(8,128)S(1)}, f32[128,512]{1,0:T(8,128)S(1)}, u32[]{:S(2)}, u32[]{:S(2)}) collective-permute-start(f32[128,512]{1,0:T(8,128)S(1)} %pad_maximum_fusion.refs_0_), channel_id=1, source_target_pairs={{0,1},{1,0},{2,3},{3,2},{4,5},{5,4},{6,7},{7,6},{8,9},{9,8},{10,11... | collective-permute-start | bytes 786440 | tf_op jit(solution)/shard_map/ppermute | solution.py:175
  14.4 1.5 %collective-permute-start.5 = (f32[128,512]{1,0:T(8,128)S(1)}, f32[128,512]{1,0:T(8,128)S(1)}, u32[]{:S(2)}, u32[]{:S(2)}) collective-permute-start(f32[128,512]{1,0:T(8,128)S(1)} %pad_maximum_fusion.refs_0_), channel_id=1, source_target_pairs={{0,2},{1,3},{2,0},{3,1},{4,6},{5,7},{6,4},{7,5},{8,10},{9,11},{10,... | collective-permute-start | bytes 786440 | tf_op jit(solution)/shard_map/ppermute | solution.py:175
  15.9 0.4 collective-permute-start.4
  16.3 2.3 %copy.13 = f32[4,16,8,512]{3,2,0,1:T(8,128)} copy(f32[4,16,8,512]{3,2,1,0:T(8,128)} %bitcast.15) | data formatting | bytes 2097152 | tf_op jit(solution)/shard_map/all_to_all | solution.py:209
  18.6 0.0 copy-start
  18.6 4.2 %all-to-all-start = ((f32[32,16,512]{2,0,1:T(8,128)}), f32[32,16,512]{2,0,1:T(8,128)S(1)}, u32[]{:S(2)}, u32[]{:S(2)}) async-start(f32[32,16,512]{2,0,1:T(8,128)} %bitcast.11), calls=%async_computation | async-start | bytes 2097152 | tf_op jit(solution)/shard_map/all_to_all | solution.py:209
  22.8 0.1 collective-permute-start.7
  22.9 0.0 collective-permute-done.6.refs_3_
  22.9 0.5 collective-permute-start.10
  23.4 0.2 collective-permute-done.5.refs_2_
  23.5 0.0 collective-permute-start.9
  23.6 0.0 collective-permute-done.4.refs_1_
  23.6 0.5 collective-permute-start.8
  24.1 0.4 collective-permute-done.7.refs_4_
  24.4 0.4 collective-permute-done.10.refs_7_
  24.8 0.4 collective-permute-done.9.refs_6_
  25.2 0.4 collective-permute-done.8.refs_5_
  25.5 0.0 copy-done
  25.5 18.2 %shard_map.74.w_ref = bf16[2,512,512]{2,1,0:T(8,128)(2,1)S(1)} custom-call(f32[128,512]{1,0:T(8,128)S(1)} %pad_maximum_fusion.refs_0_, f32[128,512]{1,0:T(8,128)S(1)} %collective-permute-done.4.refs_1_, f32[128,512]{1,0:T(8,128)S(1)} %collective-permute-done.5.refs_2_, f32[128,512]{1,0:T(8,128)S(1)} %collective-permute-done.6.refs_3_, ...), custom_call_target="tpu_custom_call" | custom-call | flops 16106127360 | bytes 2097152 | tf_op jit(solution)/shard_map/pallas_call | solution.py:137
  43.8 2.5 %all-to-all-done = f32[32,16,512]{2,0,1:T(8,128)S(1)} async-done(((f32[32,16,512]{2,0,1:T(8,128)}), f32[32,16,512]{2,0,1:T(8,128)S(1)}, u32[]{:S(2)}, u32[]{:S(2)}) %all-to-all-start) | async-done | bytes 1048608 | tf_op jit(solution)/shard_map/all_to_all | solution.py:209
  46.3 1.1 %shard_map.75 = f32[512,512]{1,0:T(8,128)S(1)} custom-call(bf16[2,512,512]{2,1,0:T(8,128)(2,1)S(1)} %shard_map.74.w_ref, f32[512,512]{1,0:T(8,128)S(1)} %bitcast.12), custom_call_target="tpu_custom_call" | custom-call | flops 805306368 | bytes 3145728 | tf_op jit(solution)/shard_map/pallas_call | solution.py:160
  47.4 33.4 %all_to_all.38 = f32[16,32,512]{2,1,0:T(8,128)S(1)} all-to-all(f32[16,32,512]{2,1,0:T(8,128)S(1)} %bitcast.13), channel_id=1, replica_groups=mesh['region'=2,'member'=16] {'member'}, dimensions={0} | all-to-all | bytes 2097152 | tf_op jit(solution)/shard_map/all_to_all | solution.py:211
  80.8 1.1 %copy.11 = f32[16,4,8,512]{3,2,0,1:T(8,128)} copy(f32[16,4,8,512]{3,2,1,0:T(8,128)S(1)} %bitcast.14) | data formatting | bytes 2097152 | tf_op jit(solution)/shard_map/all_to_all | solution.py:211
Async XLA Ops:
  0.0 7.0 %collective-permute-start.2 = (f32[32,512]{1,0:T(8,128)}, f32[32,512]{1,0:T(8,128)S(1)}, u32[]{:S(2)}, u32[]{:S(2)}) collective-permute-start(f32[32,512]{1,0:T(8,128)} %bitcast.16), channel_id=1, source_target_pairs={{0,4},{1,5},{2,6},{3,7},{4,0},{5,1},{6,2},{7,3},{8,12},{9,13},{10,... | collective-permute-start | bytes 196616 | tf_op jit(solution)/shard_map/ppermute | solution.py:175
  3.0 6.1 %collective-permute-start.1 = (f32[32,512]{1,0:T(8,128)}, f32[32,512]{1,0:T(8,128)S(1)}, u32[]{:S(2)}, u32[]{:S(2)}) collective-permute-start(f32[32,512]{1,0:T(8,128)} %bitcast.17), channel_id=1, source_target_pairs={{0,8},{1,9},{2,10},{3,11},{4,12},{5,13},{6,14},{7,15},{8,0},{9,1},... | collective-permute-start | bytes 196616 | tf_op jit(solution)/shard_map/ppermute | solution.py:175
  5.6 6.3 %collective-permute-start = (f32[32,512]{1,0:T(8,128)}, f32[32,512]{1,0:T(8,128)S(1)}, u32[]{:S(2)}, u32[]{:S(2)}) collective-permute-start(f32[32,512]{1,0:T(8,128)} %bitcast.18), channel_id=1, source_target_pairs={{0,12},{1,13},{2,14},{3,15},{4,8},{5,9},{6,10},{7,11},{8,4},{9,5},... | collective-permute-start | bytes 196616 | tf_op jit(solution)/shard_map/ppermute | solution.py:175
  7.0 5.7 %collective-permute-start.3 = (f32[8,512]{1,0:T(8,128)}, f32[8,512]{1,0:T(8,128)S(1)}, u32[]{:S(2)}, u32[]{:S(2)}) collective-permute-start(f32[8,512]{1,0:T(8,128)} %shard_map.73.refs_8_), channel_id=1, source_target_pairs={{0,16},{16,0},{1,17},{17,1},{2,18},{18,2},{3,19},{19,3},{4,20},{20... | collective-permute-start | bytes 49160 | tf_op jit(solution)/shard_map/ppermute | solution.py:182
  12.8 10.1 %collective-permute-start.6 = (f32[128,512]{1,0:T(8,128)S(1)}, f32[128,512]{1,0:T(8,128)S(1)}, u32[]{:S(2)}, u32[]{:S(2)}) collective-permute-start(f32[128,512]{1,0:T(8,128)S(1)} %pad_maximum_fusion.refs_0_), channel_id=1, source_target_pairs={{0,1},{1,0},{2,3},{3,2},{4,5},{5,4},{6,7},{7,6},{8,9},{9,8},{10,11... | collective-permute-start | bytes 786440 | tf_op jit(solution)/shard_map/ppermute | solution.py:175
  14.4 9.2 %collective-permute-start.5 = (f32[128,512]{1,0:T(8,128)S(1)}, f32[128,512]{1,0:T(8,128)S(1)}, u32[]{:S(2)}, u32[]{:S(2)}) collective-permute-start(f32[128,512]{1,0:T(8,128)S(1)} %pad_maximum_fusion.refs_0_), channel_id=1, source_target_pairs={{0,2},{1,3},{2,0},{3,1},{4,6},{5,7},{6,4},{7,5},{8,10},{9,11},{10,... | collective-permute-start | bytes 786440 | tf_op jit(solution)/shard_map/ppermute | solution.py:175
  15.9 7.7 %collective-permute-start.4 = (f32[128,512]{1,0:T(8,128)S(1)}, f32[128,512]{1,0:T(8,128)S(1)}, u32[]{:S(2)}, u32[]{:S(2)}) collective-permute-start(f32[128,512]{1,0:T(8,128)S(1)} %pad_maximum_fusion.refs_0_), channel_id=1, source_target_pairs={{0,3},{1,2},{2,1},{3,0},{4,7},{5,6},{6,5},{7,4},{8,11},{9,10},{10,... | collective-permute-start | bytes 786440 | tf_op jit(solution)/shard_map/ppermute | solution.py:175
  18.6 6.9 %copy-start = (f32[8,512]{1,0:T(8,128)S(1)}, f32[8,512]{1,0:T(8,128)}, u32[]{:S(2)}) copy-start(f32[8,512]{1,0:T(8,128)} %shard_map.73.refs_8_) | copy-start | bytes 49156
  18.6 27.7 %all-to-all-start = ((f32[32,16,512]{2,0,1:T(8,128)}), f32[32,16,512]{2,0,1:T(8,128)S(1)}, u32[]{:S(2)}, u32[]{:S(2)}) async-start(f32[32,16,512]{2,0,1:T(8,128)} %bitcast.11), calls=%async_computation | async-start | bytes 2097152 | tf_op jit(solution)/shard_map/all_to_all | solution.py:209
  22.8 1.6 %collective-permute-start.7 = (f32[128,512]{1,0:T(8,128)S(1)}, f32[128,512]{1,0:T(8,128)S(1)}, u32[]{:S(2)}, u32[]{:S(2)}) collective-permute-start(f32[128,512]{1,0:T(8,128)S(1)} %pad_maximum_fusion.refs_0_), channel_id=1, source_target_pairs={{0,16},{16,0},{1,17},{17,1},{2,18},{18,2},{3,19},{19,3},{4,20},{20... | collective-permute-start | bytes 786440 | tf_op jit(solution)/shard_map/ppermute | solution.py:182
  22.9 1.9 %collective-permute-start.10 = (f32[128,512]{1,0:T(8,128)S(1)}, f32[128,512]{1,0:T(8,128)S(1)}, u32[]{:S(2)}, u32[]{:S(2)}) collective-permute-start(f32[128,512]{1,0:T(8,128)S(1)} %collective-permute-done.6.refs_3_), channel_id=1, source_target_pairs={{0,16},{16,0},{1,17},{17,1},{2,18},{18,2},{3,19},{19,3},{4,20},{20... | collective-permute-start | bytes 786440 | tf_op jit(solution)/shard_map/ppermute | solution.py:182
  23.5 1.6 %collective-permute-start.9 = (f32[128,512]{1,0:T(8,128)S(1)}, f32[128,512]{1,0:T(8,128)S(1)}, u32[]{:S(2)}, u32[]{:S(2)}) collective-permute-start(f32[128,512]{1,0:T(8,128)S(1)} %collective-permute-done.5.refs_2_), channel_id=1, source_target_pairs={{0,16},{16,0},{1,17},{17,1},{2,18},{18,2},{3,19},{19,3},{4,20},{20... | collective-permute-start | bytes 786440 | tf_op jit(solution)/shard_map/ppermute | solution.py:182
  23.6 2.0 %collective-permute-start.8 = (f32[128,512]{1,0:T(8,128)S(1)}, f32[128,512]{1,0:T(8,128)S(1)}, u32[]{:S(2)}, u32[]{:S(2)}) collective-permute-start(f32[128,512]{1,0:T(8,128)S(1)} %collective-permute-done.4.refs_1_), channel_id=1, source_target_pairs={{0,16},{16,0},{1,17},{17,1},{2,18},{18,2},{3,19},{19,3},{4,20},{20... | collective-permute-start | bytes 786440 | tf_op jit(solution)/shard_map/ppermute | solution.py:182

commit v2 on v1

--- a/solution.py
+++ b/solution.py
@@ -35,22 +35,35 @@
     return ref[0], ref[1]
 
 
-def eye(order):
-    shape = (order, order)
+def eye(shape):
     same = lax.broadcasted_iota(jnp.int32, shape, 0) == lax.broadcasted_iota(jnp.int32, shape, 1)
     return jnp.where(same, 1.0, 0.0).astype(F32)
 
 
-def row_pair(row):
-    width = row.shape[1]
-    high, low = split(jnp.broadcast_to(row, (8, width)))
-    return jnp.concatenate([high.astype(F32), low.astype(F32)], 0).astype(BF16)
-
-
-def row_dot(row, b, dims=NN):
-    pair = row_pair(row)
-    both = dot(pair, b[0], dims) + dot(pair, b[1], dims)
-    return both[0:1] + both[8:9]
+def sym_dot(a, b, half, dims=NN, row=None):
+    upper = [a[0, :half, :], a[1, :half, :]]
+    if row is not None:
+        parts = split(jnp.broadcast_to(row, (16, row.shape[1])))
+        upper = [jnp.concatenate(pair) for pair in zip(upper, parts)]
+    corner = (slice(half, None), slice(None)) if dims is NT else (slice(None), slice(half, None))
+    top = dot3(upper, get(b), dims)
+    low = dot3(
+        (a[0, half:, :], a[1, half:, :]), (b[(0, *corner)], b[(1, *corner)]), dims
+    )
+    if row is None:
+        return top, low
+    return top[:half], low, top[half : half + 1]
+
+
+def put_at(ref, rows, cols, x):
+    ref[0, rows, cols], ref[1, rows, cols] = split(x)
+
+
+def sym_put(ref, top, low, half):
+    first, rest = slice(0, half), slice(half, None)
+    put_at(ref, first, slice(None), top)
+    put_at(ref, rest, rest, low)
+    put_at(ref, rest, first, top[:, half:].T)
 
 
 def pack_kernel(owner_ref, index_ref, innov_ref, var_ref, table_ref, o_ref):
@@ -104,29 +117,44 @@
             high, low = split(data * root[:, cols])
             s_ref[0, pl.ds(at, rows), cols] = high
             s_ref[1, pl.ds(at, rows), cols] = low
-    s = get(s_ref)
-    forcing = row_dot(root * info[2:3], s, NT)
-    system = dot3(s, s, NT) + (order - 1.0) * eye(order)
-    inv_norm = lax.rsqrt(jnp.sum(system * system))
-    first = system * inv_norm
-    put(q_ref, first)
-    put(z_ref, 1.5 * eye(order) - 0.5 * first)
-    put(q_ref, dot3(get(q_ref), get(z_ref)))
-
-    def sweep(i, carry):
-        put(u_ref, 1.5 * eye(order) - 0.5 * dot3(get(z_ref), get(q_ref)))
-        next_q = dot3(get(q_ref), get(u_ref))
-        next_z = dot3(get(u_ref), get(z_ref))
-        put(q_ref, next_q)
-        put(z_ref, next_z)
-        return carry
-
-    lax.fori_loop(0, ITERS - 2, sweep, 0)
-    put(u_ref, 1.5 * eye(order) - 0.5 * dot3(get(z_ref), get(q_ref)))
-    z = dot3(get(u_ref), get(z_ref))
-    put(z_ref, z)
-    shift = row_dot(row_dot(forcing, get(z_ref)), get(z_ref)) * inv_norm
-    put(w_ref, (jnp.sqrt(order - 1.0) * jnp.sqrt(inv_norm)) * z + shift)
+    half = order // 2
+    eye_top, eye_low = eye((half, order)), eye((half, half))
+    top, low, row = sym_dot(s_ref, s_ref, half, NT, root * info[2:3])
+    top, low = top + (order - 1.0) * eye_top, low + (order - 1.0) * eye_low
+    corner = top[:, half:]
+    inv_norm = lax.rsqrt(jnp.sum(top * top) + jnp.sum(corner * corner) + jnp.sum(low * low))
+    top, low = top * inv_norm, low * inv_norm
+    sym_put(q_ref, top, low, half)
+    sym_put(z_ref, 1.5 * eye_top - 0.5 * top, 1.5 * eye_low - 0.5 * low, half)
+
+    def put_update(top, low):
+        shape = top.shape
+        sym_put(u_ref, 1.5 * eye(shape) - 0.5 * top, 1.5 * eye(low.shape) - 0.5 * low, half)
+
+    sym_put(q_ref, *sym_dot(q_ref, z_ref, half), half)
+    for _ in range(ITERS - 2):
+        put_update(*sym_dot(q_ref, z_ref, half))
+        next_q = sym_dot(q_ref, u_ref, half)
+        next_z = sym_dot(z_ref, u_ref, half)
+        sym_put(q_ref, *next_q, half)
+        sym_put(z_ref, *next_z, half)
+    top, low, row = sym_dot(q_ref, z_ref, half, NN, row)
+    put_update(top, low)
+    top, low, row = sym_dot(z_ref, u_ref, half, NN, row)
+    left = top[:, half:].T
+    lanes = 128
+    column = jnp.broadcast_to(row, (lanes, order)).T
+    upper = jnp.concatenate([column[:half]] * (order // lanes), 1)
+    lower = jnp.concatenate([column[half:]] * (half // lanes), 1)
+    below = jnp.concatenate(
+        [jnp.sum(left * lower, 0, keepdims=True), jnp.sum(low * lower, 0, keepdims=True)], 1
+    )
+    shift = (jnp.sum(top * upper, 0, keepdims=True) + below) * inv_norm
+    gain = jnp.sqrt(order - 1.0) * jnp.sqrt(inv_norm)
+    first, rest = slice(0, half), slice(half, None)
+    put_at(w_ref, first, slice(None), gain * top + shift)
+    put_at(w_ref, rest, rest, gain * low + shift[:, half:])
+    put_at(w_ref, rest, first, gain * left + shift[:, :half])
 
 
 def solve(orders, own_parts, far_parts, own_info, far_info):
@@ -190,15 +218,15 @@
         return (same, same), [whole], [from_region(whole)], from_region(info)
     far_steps = [step * low for step in range(low)][::-1][:-1]
     near_steps = list(range(low))[::-1][:-1]
-    got = [swap_by(shard, count, a, b) for a, b in zip(far_steps, near_steps)]
+    got = [swap_by(shard, count, a, b) for a, b in zip(far_steps, far_steps)]
     held = jnp.concatenate([shard] + got)
     far_info = from_region(info)
     held, far_info = lax.optimization_barrier((held, far_info))
-    own = [held] + [swap_by(held, count, a, b) for a, b in zip(near_steps, far_steps)]
+    own = [held] + [swap_by(held, count, a, b) for a, b in zip(near_steps, near_steps)]
     far = [from_region(part) for part in own]
     far_first = [n ^ f for n in [0] + near_steps for f in [0] + far_steps]
     near_first = [f ^ n for f in [0] + far_steps for n in [0] + near_steps]
-    return (far_first, near_first), own, far, far_info
+    return (far_first, far_first), own, far, far_info
 
 
 def local(state, obs_pert, owners, loc_index, innov, obs_var, loc_scales):

time: 82.3 us -> 80.8 us (0.982)
  Pallas kernels: 20.8 us -> 16.9 us
  waiting for transfers between devices: 8.97 us -> 12 us
  blocking collectives: 33.4 us -> 31.9 us
  starting transfers between devices: 14.4 us -> 15.4 us
    ppermute x6, waiting for transfers between devices: 5.01 us -> 9.85 us  [swap_by(): return lax.ppermute(block, ('region', 'member'), route)]
    pallas_call x1, Pallas kernels: 18.2 us -> 14.4 us  [solve(): pl.pallas_call(functools.partial(solve_kernel, orders, len(operands)), ou...]
    all_to_all x1, waiting for transfers between devices: 2.48 us -> 0.73 us  [local(): lax.all_to_all(state, 'member', split_axis=1, concat_axis=0, tiled=True)]
    all_to_all x1, blocking collectives: 33.4 us -> 31.9 us  [local(): lax.all_to_all(updated, 'member', split_axis=0, concat_axis=1, tiled=True)]
    all_to_all x1, starting transfers between devices: 4.2 us -> 5.15 us  [local(): lax.all_to_all(state, 'member', split_axis=1, concat_axis=0, tiled=True)]
  transfers between devices with their start and end apart: 12 -> 12, of which waited for: 8 -> 6; matrix products, arithmetic and copies ran while one was open for 4% -> 4% of each run, Pallas kernels for 24% -> 20%
where the time goes in v2:
time: 80.8 us; the launch traced here: 80.4 us
  blocking collectives  31.9 us (39%)
  Pallas kernels  16.9 us (21%)
  starting transfers between devices  15.4 us (19%)
  waiting for transfers between devices  12 us (15%)
  local copies, waits for them, and re-layouts  3.35 us (4%)
  other arithmetic  0.86 us (1%)
    all_to_all x1, blocking collectives, local(): lax.all_to_all(updated, 'member', split_axis=0, concat_axis=1, tiled=True)  31.9 us
    pallas_call x1, Pallas kernels, solve(): pl.pallas_call(functools.partial(solve_kernel, orders, len(operands)), ou...  14.4 us
    ppermute x6, waiting for transfers between devices, swap_by(): return lax.ppermute(block, ('region', 'member'), route)  9.85 us
    ppermute x6, starting transfers between devices, swap_by(): return lax.ppermute(block, ('region', 'member'), route)  9.17 us
    all_to_all x1, starting transfers between devices, local(): lax.all_to_all(state, 'member', split_axis=1, concat_axis=0, tiled=True)  5.15 us
    all_to_all x1, local copies, waits for them, and re-layouts, local(): lax.all_to_all(state, 'member', split_axis=1, concat_axis=0, tiled=True)  2.29 us
  transfers between devices with their start and end apart: 12, of which 6 were waited for; matrix products, arithmetic and copies ran while one was open for 4% of the time, Pallas kernels for 20%

profile of v2, /device:TPU:0, one launch (start us, length us, event | category | flops | bytes accessed | tf_op | source)
XLA Modules:
  0.0 80.4 jit_solution(430438982114859564)
XLA Ops:
  0.0 3.0 %collective-permute-start.2 = (f32[32,512]{1,0:T(8,128)}, f32[32,512]{1,0:T(8,128)S(1)}, u32[]{:S(2)}, u32[]{:S(2)}) collective-permute-start(f32[32,512]{1,0:T(8,128)} %bitcast.16), channel_id=1, source_target_pairs={{0,4},{1,5},{2,6},{3,7},{4,0},{5,1},{6,2},{7,3},{8,12},{9,13},{10,... | collective-permute-start | bytes 196616 | tf_op jit(solution)/shard_map/ppermute | solution.py:203
  3.0 2.6 %collective-permute-start.1 = (f32[32,512]{1,0:T(8,128)}, f32[32,512]{1,0:T(8,128)S(1)}, u32[]{:S(2)}, u32[]{:S(2)}) collective-permute-start(f32[32,512]{1,0:T(8,128)} %bitcast.17), channel_id=1, source_target_pairs={{0,8},{1,9},{2,10},{3,11},{4,12},{5,13},{6,14},{7,15},{8,0},{9,1},... | collective-permute-start | bytes 196616 | tf_op jit(solution)/shard_map/ppermute | solution.py:203
  5.6 0.0 collective-permute-start
  5.6 1.4 %shard_map.73.refs_8_ = f32[8,512]{1,0:T(8,128)} custom-call(s32[1,512]{1,0:T(1,128)} %owner_ref.1, s32[1,512]{1,0:T(1,128)} %index_ref.1, f32[1,512]{1,0:T(1,128)} %innov_ref.1, f32[1,512]{1,0:T(1,128)} %var_ref.1, f32[8]{0:T(128)} %table_ref.1), custom_call_target="tpu_custom_call" | custom-call | tf_op jit(solution)/shard_map/pallas_call | solution.py:84
  7.0 0.0 collective-permute-start.3
  7.0 0.0 collective-permute-done.2
  7.0 3.5 %collective-permute-done.1 = f32[32,512]{1,0:T(8,128)S(1)} collective-permute-done((f32[32,512]{1,0:T(8,128)}, f32[32,512]{1,0:T(8,128)S(1)}, u32[]{:S(2)}, u32[]{:S(2)}) %collective-permute-start.1) | collective-permute-done | bytes 65568 | tf_op jit(solution)/shard_map/ppermute | solution.py:203
  10.5 1.4 %collective-permute-done = f32[32,512]{1,0:T(8,128)S(1)} collective-permute-done((f32[32,512]{1,0:T(8,128)}, f32[32,512]{1,0:T(8,128)S(1)}, u32[]{:S(2)}, u32[]{:S(2)}) %collective-permute-start) | collective-permute-done | bytes 65568 | tf_op jit(solution)/shard_map/ppermute | solution.py:203
  11.9 0.9 %pad_maximum_fusion.refs_0_ = f32[128,512]{1,0:T(8,128)S(1)} fusion(f32[32,512]{1,0:T(8,128)S(1)} %collective-permute-done.2, f32[32,512]{1,0:T(8,128)S(1)} %collective-permute-done.1, f32[32,512]{1,0:T(8,128)S(1)} %collective-permute-done, f32[32,512]{1,0:T(8,128)} %bitcast.19), kind=kLoop, calls=%fused_computation.1 | loop fusion | flops 196608 | bytes 524288 | tf_op jit(solution)/shard_map/concatenate | solution.py:222
  12.8 0.0 collective-permute-done.3.refs_9_
  12.8 1.6 %collective-permute-start.6 = (f32[128,512]{1,0:T(8,128)S(1)}, f32[128,512]{1,0:T(8,128)S(1)}, u32[]{:S(2)}, u32[]{:S(2)}) collective-permute-start(f32[128,512]{1,0:T(8,128)S(1)} %pad_maximum_fusion.refs_0_), channel_id=1, source_target_pairs={{0,1},{1,0},{2,3},{3,2},{4,5},{5,4},{6,7},{7,6},{8,9},{9,8},{10,11... | collective-permute-start | bytes 786440 | tf_op jit(solution)/shard_map/ppermute | solution.py:203
  14.3 1.5 %collective-permute-start.5 = (f32[128,512]{1,0:T(8,128)S(1)}, f32[128,512]{1,0:T(8,128)S(1)}, u32[]{:S(2)}, u32[]{:S(2)}) collective-permute-start(f32[128,512]{1,0:T(8,128)S(1)} %pad_maximum_fusion.refs_0_), channel_id=1, source_target_pairs={{0,2},{1,3},{2,0},{3,1},{4,6},{5,7},{6,4},{7,5},{8,10},{9,11},{10,... | collective-permute-start | bytes 786440 | tf_op jit(solution)/shard_map/ppermute | solution.py:203
  15.9 0.5 collective-permute-start.4
  16.3 2.3 %copy.13 = f32[4,16,8,512]{3,2,0,1:T(8,128)} copy(f32[4,16,8,512]{3,2,1,0:T(8,128)} %bitcast.15) | data formatting | bytes 2097152 | tf_op jit(solution)/shard_map/all_to_all | solution.py:237
  18.6 0.0 copy-start
  18.6 5.2 %all-to-all-start = ((f32[32,16,512]{2,0,1:T(8,128)}), f32[32,16,512]{2,0,1:T(8,128)S(1)}, u32[]{:S(2)}, u32[]{:S(2)}) async-start(f32[32,16,512]{2,0,1:T(8,128)} %bitcast.11), calls=%async_computation | async-start | bytes 2097152 | tf_op jit(solution)/shard_map/all_to_all | solution.py:237
  23.8 0.1 collective-permute-start.7
  23.9 0.0 collective-permute-done.6.refs_3_
  23.9 0.5 collective-permute-start.10
  24.4 5.0 %collective-permute-done.5.refs_2_ = f32[128,512]{1,0:T(8,128)S(1)} collective-permute-done((f32[128,512]{1,0:T(8,128)S(1)}, f32[128,512]{1,0:T(8,128)S(1)}, u32[]{:S(2)}, u32[]{:S(2)}) %collective-permute-start.5) | collective-permute-done | bytes 262176 | tf_op jit(solution)/shard_map/ppermute | solution.py:203
  29.3 0.0 collective-permute-start.9
  29.3 0.0 collective-permute-done.4.refs_1_
  29.4 0.5 collective-permute-start.8
  29.9 0.0 collective-permute-done.7.refs_4_
  29.9 0.0 collective-permute-done.10.refs_7_
  29.9 1.0 %collective-permute-done.9.refs_6_ = f32[128,512]{1,0:T(8,128)S(1)} collective-permute-done((f32[128,512]{1,0:T(8,128)S(1)}, f32[128,512]{1,0:T(8,128)S(1)}, u32[]{:S(2)}, u32[]{:S(2)}) %collective-permute-start.9) | collective-permute-done | bytes 262176 | tf_op jit(solution)/shard_map/ppermute | solution.py:210
  30.9 0.4 collective-permute-done.8.refs_5_
  31.3 0.0 copy-done
  31.3 14.4 %shard_map.74.w_ref = bf16[2,512,512]{2,1,0:T(8,128)(2,1)S(1)} custom-call(f32[128,512]{1,0:T(8,128)S(1)} %pad_maximum_fusion.refs_0_, f32[128,512]{1,0:T(8,128)S(1)} %collective-permute-done.4.refs_1_, f32[128,512]{1,0:T(8,128)S(1)} %collective-permute-done.5.refs_2_, f32[128,512]{1,0:T(8,128)S(1)} %collective-permute-done.6.refs_3_, ...), custom_call_target="tpu_custom_call" | custom-call | flops 16106127360 | bytes 2097152 | tf_op jit(solution)/shard_map/pallas_call | solution.py:165
  45.6 0.7 all-to-all-done
  46.4 1.1 %shard_map.75 = f32[512,512]{1,0:T(8,128)S(1)} custom-call(bf16[2,512,512]{2,1,0:T(8,128)(2,1)S(1)} %shard_map.74.w_ref, f32[512,512]{1,0:T(8,128)S(1)} %bitcast.12), custom_call_target="tpu_custom_call" | custom-call | flops 805306368 | bytes 3145728 | tf_op jit(solution)/shard_map/pallas_call | solution.py:188
  47.5 31.9 %all_to_all.38 = f32[16,32,512]{2,1,0:T(8,128)S(1)} all-to-all(f32[16,32,512]{2,1,0:T(8,128)S(1)} %bitcast.13), channel_id=1, replica_groups=mesh['region'=2,'member'=16] {'member'}, dimensions={0} | all-to-all | bytes 2097152 | tf_op jit(solution)/shard_map/all_to_all | solution.py:239
  79.4 1.1 %copy.11 = f32[16,4,8,512]{3,2,0,1:T(8,128)} copy(f32[16,4,8,512]{3,2,1,0:T(8,128)S(1)} %bitcast.14) | data formatting | bytes 2097152 | tf_op jit(solution)/shard_map/all_to_all | solution.py:239
Async XLA Ops:
  0.0 7.0 %collective-permute-start.2 = (f32[32,512]{1,0:T(8,128)}, f32[32,512]{1,0:T(8,128)S(1)}, u32[]{:S(2)}, u32[]{:S(2)}) collective-permute-start(f32[32,512]{1,0:T(8,128)} %bitcast.16), channel_id=1, source_target_pairs={{0,4},{1,5},{2,6},{3,7},{4,0},{5,1},{6,2},{7,3},{8,12},{9,13},{10,... | collective-permute-start | bytes 196616 | tf_op jit(solution)/shard_map/ppermute | solution.py:203
  3.0 7.5 %collective-permute-start.1 = (f32[32,512]{1,0:T(8,128)}, f32[32,512]{1,0:T(8,128)S(1)}, u32[]{:S(2)}, u32[]{:S(2)}) collective-permute-start(f32[32,512]{1,0:T(8,128)} %bitcast.17), channel_id=1, source_target_pairs={{0,8},{1,9},{2,10},{3,11},{4,12},{5,13},{6,14},{7,15},{8,0},{9,1},... | collective-permute-start | bytes 196616 | tf_op jit(solution)/shard_map/ppermute | solution.py:203
  5.6 6.3 %collective-permute-start = (f32[32,512]{1,0:T(8,128)}, f32[32,512]{1,0:T(8,128)S(1)}, u32[]{:S(2)}, u32[]{:S(2)}) collective-permute-start(f32[32,512]{1,0:T(8,128)} %bitcast.18), channel_id=1, source_target_pairs={{0,12},{1,13},{2,14},{3,15},{4,8},{5,9},{6,10},{7,11},{8,4},{9,5},... | collective-permute-start | bytes 196616 | tf_op jit(solution)/shard_map/ppermute | solution.py:203
  7.0 5.7 %collective-permute-start.3 = (f32[8,512]{1,0:T(8,128)}, f32[8,512]{1,0:T(8,128)S(1)}, u32[]{:S(2)}, u32[]{:S(2)}) collective-permute-start(f32[8,512]{1,0:T(8,128)} %shard_map.73.refs_8_), channel_id=1, source_target_pairs={{0,16},{16,0},{1,17},{17,1},{2,18},{18,2},{3,19},{19,3},{4,20},{20... | collective-permute-start | bytes 49160 | tf_op jit(solution)/shard_map/ppermute | solution.py:210
  12.8 11.1 %collective-permute-start.6 = (f32[128,512]{1,0:T(8,128)S(1)}, f32[128,512]{1,0:T(8,128)S(1)}, u32[]{:S(2)}, u32[]{:S(2)}) collective-permute-start(f32[128,512]{1,0:T(8,128)S(1)} %pad_maximum_fusion.refs_0_), channel_id=1, source_target_pairs={{0,1},{1,0},{2,3},{3,2},{4,5},{5,4},{6,7},{7,6},{8,9},{9,8},{10,11... | collective-permute-start | bytes 786440 | tf_op jit(solution)/shard_map/ppermute | solution.py:203
  14.3 15.0 %collective-permute-start.5 = (f32[128,512]{1,0:T(8,128)S(1)}, f32[128,512]{1,0:T(8,128)S(1)}, u32[]{:S(2)}, u32[]{:S(2)}) collective-permute-start(f32[128,512]{1,0:T(8,128)S(1)} %pad_maximum_fusion.refs_0_), channel_id=1, source_target_pairs={{0,2},{1,3},{2,0},{3,1},{4,6},{5,7},{6,4},{7,5},{8,10},{9,11},{10,... | collective-permute-start | bytes 786440 | tf_op jit(solution)/shard_map/ppermute | solution.py:203
  15.9 13.5 %collective-permute-start.4 = (f32[128,512]{1,0:T(8,128)S(1)}, f32[128,512]{1,0:T(8,128)S(1)}, u32[]{:S(2)}, u32[]{:S(2)}) collective-permute-start(f32[128,512]{1,0:T(8,128)S(1)} %pad_maximum_fusion.refs_0_), channel_id=1, source_target_pairs={{0,3},{1,2},{2,1},{3,0},{4,7},{5,6},{6,5},{7,4},{8,11},{9,10},{10,... | collective-permute-start | bytes 786440 | tf_op jit(solution)/shard_map/ppermute | solution.py:203
  18.6 12.6 %copy-start = (f32[8,512]{1,0:T(8,128)S(1)}, f32[8,512]{1,0:T(8,128)}, u32[]{:S(2)}) copy-start(f32[8,512]{1,0:T(8,128)} %shard_map.73.refs_8_) | copy-start | bytes 49156
  18.6 27.7 %all-to-all-start = ((f32[32,16,512]{2,0,1:T(8,128)}), f32[32,16,512]{2,0,1:T(8,128)S(1)}, u32[]{:S(2)}, u32[]{:S(2)}) async-start(f32[32,16,512]{2,0,1:T(8,128)} %bitcast.11), calls=%async_computation | async-start | bytes 2097152 | tf_op jit(solution)/shard_map/all_to_all | solution.py:237
  23.8 6.1 %collective-permute-start.7 = (f32[128,512]{1,0:T(8,128)S(1)}, f32[128,512]{1,0:T(8,128)S(1)}, u32[]{:S(2)}, u32[]{:S(2)}) collective-permute-start(f32[128,512]{1,0:T(8,128)S(1)} %pad_maximum_fusion.refs_0_), channel_id=1, source_target_pairs={{0,16},{16,0},{1,17},{17,1},{2,18},{18,2},{3,19},{19,3},{4,20},{20... | collective-permute-start | bytes 786440 | tf_op jit(solution)/shard_map/ppermute | solution.py:210
  23.9 6.0 %collective-permute-start.10 = (f32[128,512]{1,0:T(8,128)S(1)}, f32[128,512]{1,0:T(8,128)S(1)}, u32[]{:S(2)}, u32[]{:S(2)}) collective-permute-start(f32[128,512]{1,0:T(8,128)S(1)} %collective-permute-done.6.refs_3_), channel_id=1, source_target_pairs={{0,16},{16,0},{1,17},{17,1},{2,18},{18,2},{3,19},{19,3},{4,20},{20... | collective-permute-start | bytes 786440 | tf_op jit(solution)/shard_map/ppermute | solution.py:210
  29.3 1.5 %collective-permute-start.9 = (f32[128,512]{1,0:T(8,128)S(1)}, f32[128,512]{1,0:T(8,128)S(1)}, u32[]{:S(2)}, u32[]{:S(2)}) collective-permute-start(f32[128,512]{1,0:T(8,128)S(1)} %collective-permute-done.5.refs_2_), channel_id=1, source_target_pairs={{0,16},{16,0},{1,17},{17,1},{2,18},{18,2},{3,19},{19,3},{4,20},{20... | collective-permute-start | bytes 786440 | tf_op jit(solution)/shard_map/ppermute | solution.py:210
  29.4 1.9 %collective-permute-start.8 = (f32[128,512]{1,0:T(8,128)S(1)}, f32[128,512]{1,0:T(8,128)S(1)}, u32[]{:S(2)}, u32[]{:S(2)}) collective-permute-start(f32[128,512]{1,0:T(8,128)S(1)} %collective-permute-done.4.refs_1_), channel_id=1, source_target_pairs={{0,16},{16,0},{1,17},{17,1},{2,18},{18,2},{3,19},{19,3},{4,20},{20... | collective-permute-start | bytes 786440 | tf_op jit(solution)/shard_map/ppermute | solution.py:210

commit v3 on v2

--- a/solution.py
+++ b/solution.py
@@ -89,37 +89,43 @@
     )(owners, loc_index, innov, obs_var, loc_scales)
 
 
-def solve_kernel(orders, count, *refs):
-    nparts = (count - 2) // 2
-    own_refs, far_refs = refs[:nparts], refs[nparts : 2 * nparts]
-    own_info, far_info, w_ref, s_ref, z_ref, q_ref, u_ref = refs[2 * nparts :]
-    order = w_ref.shape[1]
-    nobs = own_info.shape[1]
-    blocks = len(orders[0])
-    rows = order // blocks
+def region_gram(orders, r, part_refs, info_ref, s_ref):
+    order, nobs = s_ref.shape[1:]
+    blocks, nparts = len(orders[0]), len(part_refs)
+    rows, per_part = order // blocks, blocks // nparts
     region, member = lax.axis_index("region"), lax.axis_index("member")
     nmember = lax.axis_size("member")
     patch = (region * nmember + member).astype(F32)
     cycle = float(nmember * lax.axis_size("region"))
-    info = jnp.concatenate([own_info[...], far_info[...]], axis=1)
-    dist = jnp.abs(patch - info[0:1])
-    ratio = jnp.minimum(dist, cycle - dist) / info[1:2]
-    root = jnp.exp(-0.5 * ratio * ratio) * lax.rsqrt(info[3:4])
-    for r, parts in enumerate((own_refs, far_refs)):
-        cols = slice(r * nobs, (r + 1) * nobs)
-        per_part = blocks // nparts
-        for p in range(blocks):
-            offset = jnp.where(region == r, orders[0][p], orders[1][p])
-            block = member ^ offset if nparts > 1 else offset
-            at = pl.multiple_of(block * rows, rows)
-            place = p % per_part * rows
-            data = parts[p // per_part][place : place + rows, :]
-            high, low = split(data * root[:, cols])
-            s_ref[0, pl.ds(at, rows), cols] = high
-            s_ref[1, pl.ds(at, rows), cols] = low
+    dist = jnp.abs(patch - info_ref[0:1])
+    ratio = jnp.minimum(dist, cycle - dist) / info_ref[1:2]
+    root = jnp.exp(-0.5 * ratio * ratio) * lax.rsqrt(info_ref[3:4])
+    for p in range(blocks):
+        offset = jnp.where(region == r, orders[0][p], orders[1][p])
+        block = member ^ offset if nparts > 1 else offset
+        at = pl.multiple_of(block * rows, rows)
+        place = p % per_part * rows
+        high, low = split(part_refs[p // per_part][place : place + rows, :] * root)
+        s_ref[0, pl.ds(at, rows), :] = high
+        s_ref[1, pl.ds(at, rows), :] = low
+    return sym_dot(s_ref, s_ref, order // 2, NT, root * info_ref[2:3])
+
+
+def gram_kernel(orders, nparts, *refs):
+    info_ref, top_ref, low_ref, row_ref, s_ref = refs[nparts:]
+    top, low, row = region_gram(orders, 0, refs[:nparts], info_ref, s_ref)
+    top_ref[...] = top
+    low_ref[...] = low
+    row_ref[...] = jnp.broadcast_to(row, row_ref.shape)
+
+
+def solve_kernel(orders, nparts, *refs):
+    info_ref, own_top, own_low, own_row, w_ref, s_ref, z_ref, q_ref, u_ref = refs[nparts:]
+    order = w_ref.shape[1]
+    top, low, row = region_gram(orders, 1, refs[:nparts], info_ref, s_ref)
+    top, low, row = top + own_top[...], low + own_low[...], row + own_row[0:1]
     half = order // 2
     eye_top, eye_low = eye((half, order)), eye((half, half))
-    top, low, row = sym_dot(s_ref, s_ref, half, NT, root * info[2:3])
     top, low = top + (order - 1.0) * eye_top, low + (order - 1.0) * eye_low
     corner = top[:, half:]
     inv_norm = lax.rsqrt(jnp.sum(top * top) + jnp.sum(corner * corner) + jnp.sum(low * low))
@@ -160,20 +166,33 @@
 def solve(orders, own_parts, far_parts, own_info, far_info):
     order = sum(part.shape[0] for part in own_parts)
     nobs = own_parts[0].shape[1]
+    half = order // 2
     vmem = pl.BlockSpec(memory_space=pltpu.VMEM)
-    operands = [*own_parts, *far_parts, own_info, far_info]
+    pair = pltpu.VMEM((2, order, order), BF16)
+    nparts = len(own_parts)
+    shapes = [(half, order), (half, half), (8, order)]
+    own = pl.pallas_call(
+        functools.partial(gram_kernel, orders, nparts),
+        out_shape=[jax.ShapeDtypeStruct(shape, F32) for shape in shapes],
+        in_specs=[vmem] * (nparts + 1),
+        out_specs=[vmem] * 3,
+        scratch_shapes=[pltpu.VMEM((2, order, nobs), BF16)],
+        compiler_params=pltpu.CompilerParams(vmem_limit_bytes=24 << 20),
+        cost_estimate=pl.CostEstimate(
+            flops=3 * 2 * order**3, bytes_accessed=4 * order * nobs, transcendentals=0
+        ),
+    )(*own_parts, own_info)
     return pl.pallas_call(
-        functools.partial(solve_kernel, orders, len(operands)),
+        functools.partial(solve_kernel, orders, nparts),
         out_shape=jax.ShapeDtypeStruct((2, order, order), BF16),
-        in_specs=[vmem] * len(operands),
+        in_specs=[vmem] * (nparts + 4),
         out_specs=vmem,
-        scratch_shapes=[pltpu.VMEM((2, order, 2 * nobs), BF16)]
-        + [pltpu.VMEM((2, order, order), BF16)] * 3,
+        scratch_shapes=[pltpu.VMEM((2, order, nobs), BF16), pair, pair, pair],
         compiler_params=pltpu.CompilerParams(vmem_limit_bytes=40 << 20),
         cost_estimate=pl.CostEstimate(
-            flops=20 * 3 * 2 * order**3, bytes_accessed=8 * order * nobs, transcendentals=0
+            flops=21 * 3 * 2 * order**3, bytes_accessed=4 * order * nobs, transcendentals=0
         ),
-    )(*operands)
+    )(*far_parts, far_info, *own)
 
 
 def update_kernel(w_ref, x_ref, o_ref):

time: 80.8 us -> 80 us (0.990)
  blocking collectives: 31.9 us -> 31 us
    ppermute x5, waiting for transfers between devices: 1.4 us -> 0.33 us  [from_region(): return lax.ppermute(block, 'region', REGIONS)]
    all_to_all x1, waiting for transfers between devices: 0.73 us -> 1.63 us  [local(): lax.all_to_all(state, 'member', split_axis=1, concat_axis=0, tiled=True)]
    all_to_all x1, blocking collectives: 31.9 us -> 31 us  [local(): lax.all_to_all(updated, 'member', split_axis=0, concat_axis=1, tiled=True)]
    pallas_call x1 -> x2, Pallas kernels: 14.4 us -> 14.5 us  [the longest x1 13.5 us: solve(): pl.pallas_call(functools.partial(solve_kernel, orders, nparts), out_shape...]
  transfers between devices with their start and end apart: 12 -> 12, of which waited for: 6 -> 5; matrix products, arithmetic and copies ran while one was open for 4% -> 4% of each run, Pallas kernels for 20% -> 20%
where the time goes in v3:
time: 80 us; the launch traced here: 79.6 us
  blocking collectives  31 us (39%)
  Pallas kernels  17.1 us (21%)
  starting transfers between devices  15.4 us (19%)
  waiting for transfers between devices  11.8 us (15%)
  local copies, waits for them, and re-layouts  3.35 us (4%)
  other arithmetic  0.86 us (1%)
    all_to_all x1, blocking collectives, local(): lax.all_to_all(updated, 'member', split_axis=0, concat_axis=1, tiled=True)  31 us
    pallas_call x1, Pallas kernels, solve(): pl.pallas_call(functools.partial(solve_kernel, orders, nparts), out_shape...  13.5 us
    ppermute x6, waiting for transfers between devices, swap_by(): return lax.ppermute(block, ('region', 'member'), route)  9.86 us
    ppermute x6, starting transfers between devices, swap_by(): return lax.ppermute(block, ('region', 'member'), route)  9.17 us
    all_to_all x1, starting transfers between devices, local(): lax.all_to_all(state, 'member', split_axis=1, concat_axis=0, tiled=True)  5.15 us
    all_to_all x1, local copies, waits for them, and re-layouts, local(): lax.all_to_all(state, 'member', split_axis=1, concat_axis=0, tiled=True)  2.29 us
    all_to_all x1, waiting for transfers between devices, local(): lax.all_to_all(state, 'member', split_axis=1, concat_axis=0, tiled=True)  1.63 us
  transfers between devices with their start and end apart: 12, of which 5 were waited for; matrix products, arithmetic and copies ran while one was open for 4% of the time, Pallas kernels for 20%

profile of v3, /device:TPU:0, one launch (start us, length us, event | category | flops | bytes accessed | tf_op | source)
XLA Modules:
  0.0 79.6 jit_solution(14869284486665356529)
XLA Ops:
  0.0 3.0 %collective-permute-start.2 = (f32[32,512]{1,0:T(8,128)}, f32[32,512]{1,0:T(8,128)S(1)}, u32[]{:S(2)}, u32[]{:S(2)}) collective-permute-start(f32[32,512]{1,0:T(8,128)} %bitcast.16), channel_id=1, source_target_pairs={{0,4},{1,5},{2,6},{3,7},{4,0},{5,1},{6,2},{7,3},{8,12},{9,13},{10,... | collective-permute-start | bytes 196616 | tf_op jit(solution)/shard_map/ppermute | solution.py:222
  3.0 2.6 %collective-permute-start.1 = (f32[32,512]{1,0:T(8,128)}, f32[32,512]{1,0:T(8,128)S(1)}, u32[]{:S(2)}, u32[]{:S(2)}) collective-permute-start(f32[32,512]{1,0:T(8,128)} %bitcast.17), channel_id=1, source_target_pairs={{0,8},{1,9},{2,10},{3,11},{4,12},{5,13},{6,14},{7,15},{8,0},{9,1},... | collective-permute-start | bytes 196616 | tf_op jit(solution)/shard_map/ppermute | solution.py:222
  5.6 0.0 collective-permute-start
  5.6 1.4 %shard_map.73.refs_4_ = f32[8,512]{1,0:T(8,128)} custom-call(s32[1,512]{1,0:T(1,128)} %owner_ref.1, s32[1,512]{1,0:T(1,128)} %index_ref.1, f32[1,512]{1,0:T(1,128)} %innov_ref.1, f32[1,512]{1,0:T(1,128)} %var_ref.1, f32[8]{0:T(128)} %table_ref.1), custom_call_target="tpu_custom_call" | custom-call | tf_op jit(solution)/shard_map/pallas_call | solution.py:84
  7.0 0.0 collective-permute-start.3
  7.0 0.0 collective-permute-done.2
  7.0 3.5 %collective-permute-done.1 = f32[32,512]{1,0:T(8,128)S(1)} collective-permute-done((f32[32,512]{1,0:T(8,128)}, f32[32,512]{1,0:T(8,128)S(1)}, u32[]{:S(2)}, u32[]{:S(2)}) %collective-permute-start.1) | collective-permute-done | bytes 65568 | tf_op jit(solution)/shard_map/ppermute | solution.py:222
  10.5 1.4 %collective-permute-done = f32[32,512]{1,0:T(8,128)S(1)} collective-permute-done((f32[32,512]{1,0:T(8,128)}, f32[32,512]{1,0:T(8,128)S(1)}, u32[]{:S(2)}, u32[]{:S(2)}) %collective-permute-start) | collective-permute-done | bytes 65568 | tf_op jit(solution)/shard_map/ppermute | solution.py:222
  11.9 0.9 %pad_maximum_fusion.refs_0_ = f32[128,512]{1,0:T(8,128)S(1)} fusion(f32[32,512]{1,0:T(8,128)S(1)} %collective-permute-done.2, f32[32,512]{1,0:T(8,128)S(1)} %collective-permute-done.1, f32[32,512]{1,0:T(8,128)S(1)} %collective-permute-done, f32[32,512]{1,0:T(8,128)} %bitcast.19), kind=kLoop, calls=%fused_computation.1 | loop fusion | flops 196608 | bytes 524288 | tf_op jit(solution)/shard_map/concatenate | solution.py:241
  12.8 0.0 collective-permute-done.3.refs_4_
  12.8 1.6 %collective-permute-start.9 = (f32[128,512]{1,0:T(8,128)S(1)}, f32[128,512]{1,0:T(8,128)S(1)}, u32[]{:S(2)}, u32[]{:S(2)}) collective-permute-start(f32[128,512]{1,0:T(8,128)S(1)} %pad_maximum_fusion.refs_0_), channel_id=1, source_target_pairs={{0,1},{1,0},{2,3},{3,2},{4,5},{5,4},{6,7},{7,6},{8,9},{9,8},{10,11... | collective-permute-start | bytes 786440 | tf_op jit(solution)/shard_map/ppermute | solution.py:222
  14.3 1.5 %collective-permute-start.7 = (f32[128,512]{1,0:T(8,128)S(1)}, f32[128,512]{1,0:T(8,128)S(1)}, u32[]{:S(2)}, u32[]{:S(2)}) collective-permute-start(f32[128,512]{1,0:T(8,128)S(1)} %pad_maximum_fusion.refs_0_), channel_id=1, source_target_pairs={{0,2},{1,3},{2,0},{3,1},{4,6},{5,7},{6,4},{7,5},{8,10},{9,11},{10,... | collective-permute-start | bytes 786440 | tf_op jit(solution)/shard_map/ppermute | solution.py:222
  15.9 0.5 collective-permute-start.5
  16.3 2.3 %copy.13 = f32[4,16,8,512]{3,2,0,1:T(8,128)} copy(f32[4,16,8,512]{3,2,1,0:T(8,128)} %bitcast.15) | data formatting | bytes 2097152 | tf_op jit(solution)/shard_map/all_to_all | solution.py:256
  18.6 0.0 copy-start
  18.6 5.2 %all-to-all-start = ((f32[32,16,512]{2,0,1:T(8,128)}), f32[32,16,512]{2,0,1:T(8,128)S(1)}, u32[]{:S(2)}, u32[]{:S(2)}) async-start(f32[32,16,512]{2,0,1:T(8,128)} %bitcast.11), calls=%async_computation | async-start | bytes 2097152 | tf_op jit(solution)/shard_map/all_to_all | solution.py:256
  23.8 0.1 collective-permute-start.4
  23.9 0.0 collective-permute-done.9.refs_3_
  23.9 0.5 collective-permute-start.10
  24.4 5.0 %collective-permute-done.7.refs_2_ = f32[128,512]{1,0:T(8,128)S(1)} collective-permute-done((f32[128,512]{1,0:T(8,128)S(1)}, f32[128,512]{1,0:T(8,128)S(1)}, u32[]{:S(2)}, u32[]{:S(2)}) %collective-permute-start.7) | collective-permute-done | bytes 262176 | tf_op jit(solution)/shard_map/ppermute | solution.py:222
  29.3 0.0 collective-permute-start.8
  29.3 0.0 collective-permute-done.5.refs_1_
  29.4 0.5 collective-permute-start.6
  29.9 0.0 copy-done
  29.9 1.0 %shard_map.74 = (f32[256,512]{1,0:T(8,128)S(1)}, f32[256,256]{1,0:T(8,128)S(1)}, f32[8,512]{1,0:T(8,128)S(1)}) custom-call(f32[128,512]{1,0:T(8,128)S(1)} %pad_maximum_fusion.refs_0_, f32[128,512]{1,0:T(8,128)S(1)} %collective-permute-done.5.refs_1_, f32[128,512]{1,0:T(8,128)S(1)} %collective-permute-done.7.refs_2_, ...), custom_call_target="tpu_custom_call" | custom-call | flops 805306368 | bytes 1048576 | tf_op jit(solution)/shard_map/pallas_call | solution.py:174
  30.9 0.0 collective-permute-done.4.refs_0_
  30.9 0.0 collective-permute-done.10.refs_3_
  30.9 0.0 collective-permute-done.8.refs_2_
  30.9 0.3 collective-permute-done.6.refs_1_
  31.3 13.5 %shard_map.75.w_ref = bf16[2,512,512]{2,1,0:T(8,128)(2,1)S(1)} custom-call(f32[128,512]{1,0:T(8,128)S(1)} %collective-permute-done.4.refs_0_, f32[128,512]{1,0:T(8,128)S(1)} %collective-permute-done.6.refs_1_, f32[128,512]{1,0:T(8,128)S(1)} %collective-permute-done.8.refs_2_, f32[128,512]{1,0:T(8,128)S(1)} %collective-permute-done.10.refs_3_, ...), custom_call_target="tpu_custom_call" | custom-call | flops 16911433728 | bytes 1048576 | tf_op jit(solution)/shard_map/pallas_call | solution.py:185
  44.8 1.6 %all-to-all-done = f32[32,16,512]{2,0,1:T(8,128)S(1)} async-done(((f32[32,16,512]{2,0,1:T(8,128)}), f32[32,16,512]{2,0,1:T(8,128)S(1)}, u32[]{:S(2)}, u32[]{:S(2)}) %all-to-all-start) | async-done | bytes 1048608 | tf_op jit(solution)/shard_map/all_to_all | solution.py:256
  46.4 1.1 %shard_map.76 = f32[512,512]{1,0:T(8,128)S(1)} custom-call(bf16[2,512,512]{2,1,0:T(8,128)(2,1)S(1)} %shard_map.75.w_ref, f32[512,512]{1,0:T(8,128)S(1)} %bitcast.12), custom_call_target="tpu_custom_call" | custom-call | flops 805306368 | bytes 3145728 | tf_op jit(solution)/shard_map/pallas_call | solution.py:207
  47.5 31.0 %all_to_all.38 = f32[16,32,512]{2,1,0:T(8,128)S(1)} all-to-all(f32[16,32,512]{2,1,0:T(8,128)S(1)} %bitcast.13), channel_id=1, replica_groups=mesh['region'=2,'member'=16] {'member'}, dimensions={0} | all-to-all | bytes 2097152 | tf_op jit(solution)/shard_map/all_to_all | solution.py:258
  78.5 1.1 %copy.11 = f32[16,4,8,512]{3,2,0,1:T(8,128)} copy(f32[16,4,8,512]{3,2,1,0:T(8,128)S(1)} %bitcast.14) | data formatting | bytes 2097152 | tf_op jit(solution)/shard_map/all_to_all | solution.py:258
Async XLA Ops:
  0.0 7.0 %collective-permute-start.2 = (f32[32,512]{1,0:T(8,128)}, f32[32,512]{1,0:T(8,128)S(1)}, u32[]{:S(2)}, u32[]{:S(2)}) collective-permute-start(f32[32,512]{1,0:T(8,128)} %bitcast.16), channel_id=1, source_target_pairs={{0,4},{1,5},{2,6},{3,7},{4,0},{5,1},{6,2},{7,3},{8,12},{9,13},{10,... | collective-permute-start | bytes 196616 | tf_op jit(solution)/shard_map/ppermute | solution.py:222
  3.0 7.5 %collective-permute-start.1 = (f32[32,512]{1,0:T(8,128)}, f32[32,512]{1,0:T(8,128)S(1)}, u32[]{:S(2)}, u32[]{:S(2)}) collective-permute-start(f32[32,512]{1,0:T(8,128)} %bitcast.17), channel_id=1, source_target_pairs={{0,8},{1,9},{2,10},{3,11},{4,12},{5,13},{6,14},{7,15},{8,0},{9,1},... | collective-permute-start | bytes 196616 | tf_op jit(solution)/shard_map/ppermute | solution.py:222
  5.6 6.3 %collective-permute-start = (f32[32,512]{1,0:T(8,128)}, f32[32,512]{1,0:T(8,128)S(1)}, u32[]{:S(2)}, u32[]{:S(2)}) collective-permute-start(f32[32,512]{1,0:T(8,128)} %bitcast.18), channel_id=1, source_target_pairs={{0,12},{1,13},{2,14},{3,15},{4,8},{5,9},{6,10},{7,11},{8,4},{9,5},... | collective-permute-start | bytes 196616 | tf_op jit(solution)/shard_map/ppermute | solution.py:222
  7.0 5.8 %collective-permute-start.3 = (f32[8,512]{1,0:T(8,128)}, f32[8,512]{1,0:T(8,128)S(1)}, u32[]{:S(2)}, u32[]{:S(2)}) collective-permute-start(f32[8,512]{1,0:T(8,128)} %shard_map.73.refs_4_), channel_id=1, source_target_pairs={{0,16},{16,0},{1,17},{17,1},{2,18},{18,2},{3,19},{19,3},{4,20},{20... | collective-permute-start | bytes 49160 | tf_op jit(solution)/shard_map/ppermute | solution.py:229
  12.8 11.1 %collective-permute-start.9 = (f32[128,512]{1,0:T(8,128)S(1)}, f32[128,512]{1,0:T(8,128)S(1)}, u32[]{:S(2)}, u32[]{:S(2)}) collective-permute-start(f32[128,512]{1,0:T(8,128)S(1)} %pad_maximum_fusion.refs_0_), channel_id=1, source_target_pairs={{0,1},{1,0},{2,3},{3,2},{4,5},{5,4},{6,7},{7,6},{8,9},{9,8},{10,11... | collective-permute-start | bytes 786440 | tf_op jit(solution)/shard_map/ppermute | solution.py:222
  14.3 15.0 %collective-permute-start.7 = (f32[128,512]{1,0:T(8,128)S(1)}, f32[128,512]{1,0:T(8,128)S(1)}, u32[]{:S(2)}, u32[]{:S(2)}) collective-permute-start(f32[128,512]{1,0:T(8,128)S(1)} %pad_maximum_fusion.refs_0_), channel_id=1, source_target_pairs={{0,2},{1,3},{2,0},{3,1},{4,6},{5,7},{6,4},{7,5},{8,10},{9,11},{10,... | collective-permute-start | bytes 786440 | tf_op jit(solution)/shard_map/ppermute | solution.py:222
  15.9 13.5 %collective-permute-start.5 = (f32[128,512]{1,0:T(8,128)S(1)}, f32[128,512]{1,0:T(8,128)S(1)}, u32[]{:S(2)}, u32[]{:S(2)}) collective-permute-start(f32[128,512]{1,0:T(8,128)S(1)} %pad_maximum_fusion.refs_0_), channel_id=1, source_target_pairs={{0,3},{1,2},{2,1},{3,0},{4,7},{5,6},{6,5},{7,4},{8,11},{9,10},{10,... | collective-permute-start | bytes 786440 | tf_op jit(solution)/shard_map/ppermute | solution.py:222
  18.6 11.2 %copy-start = (f32[8,512]{1,0:T(8,128)S(1)}, f32[8,512]{1,0:T(8,128)}, u32[]{:S(2)}) copy-start(f32[8,512]{1,0:T(8,128)} %shard_map.73.refs_4_) | copy-start | bytes 49156
  18.6 27.7 %all-to-all-start = ((f32[32,16,512]{2,0,1:T(8,128)}), f32[32,16,512]{2,0,1:T(8,128)S(1)}, u32[]{:S(2)}, u32[]{:S(2)}) async-start(f32[32,16,512]{2,0,1:T(8,128)} %bitcast.11), calls=%async_computation | async-start | bytes 2097152 | tf_op jit(solution)/shard_map/all_to_all | solution.py:256
  23.8 7.1 %collective-permute-start.4 = (f32[128,512]{1,0:T(8,128)S(1)}, f32[128,512]{1,0:T(8,128)S(1)}, u32[]{:S(2)}, u32[]{:S(2)}) collective-permute-start(f32[128,512]{1,0:T(8,128)S(1)} %pad_maximum_fusion.refs_0_), channel_id=1, source_target_pairs={{0,16},{16,0},{1,17},{17,1},{2,18},{18,2},{3,19},{19,3},{4,20},{20... | collective-permute-start | bytes 786440 | tf_op jit(solution)/shard_map/ppermute | solution.py:229
  23.9 7.0 %collective-permute-start.10 = (f32[128,512]{1,0:T(8,128)S(1)}, f32[128,512]{1,0:T(8,128)S(1)}, u32[]{:S(2)}, u32[]{:S(2)}) collective-permute-start(f32[128,512]{1,0:T(8,128)S(1)} %collective-permute-done.9.refs_3_), channel_id=1, source_target_pairs={{0,16},{16,0},{1,17},{17,1},{2,18},{18,2},{3,19},{19,3},{4,20},{20... | collective-permute-start | bytes 786440 | tf_op jit(solution)/shard_map/ppermute | solution.py:229
  29.3 1.6 %collective-permute-start.8 = (f32[128,512]{1,0:T(8,128)S(1)}, f32[128,512]{1,0:T(8,128)S(1)}, u32[]{:S(2)}, u32[]{:S(2)}) collective-permute-start(f32[128,512]{1,0:T(8,128)S(1)} %collective-permute-done.7.refs_2_), channel_id=1, source_target_pairs={{0,16},{16,0},{1,17},{17,1},{2,18},{18,2},{3,19},{19,3},{4,20},{20... | collective-permute-start | bytes 786440 | tf_op jit(solution)/shard_map/ppermute | solution.py:229
  29.4 1.9 %collective-permute-start.6 = (f32[128,512]{1,0:T(8,128)S(1)}, f32[128,512]{1,0:T(8,128)S(1)}, u32[]{:S(2)}, u32[]{:S(2)}) collective-permute-start(f32[128,512]{1,0:T(8,128)S(1)} %collective-permute-done.5.refs_1_), channel_id=1, source_target_pairs={{0,16},{16,0},{1,17},{17,1},{2,18},{18,2},{3,19},{19,3},{4,20},{20... | collective-permute-start | bytes 786440 | tf_op jit(solution)/shard_map/ppermute | solution.py:229

commit v4 on v3

--- a/solution.py
+++ b/solution.py
@@ -229,32 +229,35 @@
     return lax.ppermute(block, "region", REGIONS)
 
 
-def gather_rows(shard, info, count):
+def gather_rows(shard, facts, blocks, count):
     low = 1 << (count.bit_length() - 1) // 2
-    if low * low != count or shard.shape[0] % 16:
+    if low != 4 or low * low != count or shard.shape[0] % 16:
         whole = lax.all_gather(shard, "member", axis=0, tiled=True)
         same = list(range(whole.shape[0] // 32))
-        return (same, same), [whole], [from_region(whole)], from_region(info)
-    far_steps = [step * low for step in range(low)][::-1][:-1]
-    near_steps = list(range(low))[::-1][:-1]
+        info = pack(*facts)
+        return (same, same), [whole], [from_region(whole)], info, from_region(info), blocks
+    far_steps = [2 * low, low, 3 * low]
+    near_steps = [2, 1, 3]
     got = [swap_by(shard, count, a, b) for a, b in zip(far_steps, far_steps)]
     held = jnp.concatenate([shard] + got)
-    far_info = from_region(info)
-    held, far_info = lax.optimization_barrier((held, far_info))
+    held, facts, blocks = lax.optimization_barrier((held, facts, blocks))
+    info, blocks = lax.optimization_barrier((pack(*facts), blocks))
     own = [held] + [swap_by(held, count, a, b) for a, b in zip(near_steps, near_steps)]
     far = [from_region(part) for part in own]
     far_first = [n ^ f for n in [0] + near_steps for f in [0] + far_steps]
     near_first = [f ^ n for f in [0] + far_steps for n in [0] + near_steps]
-    return (far_first, far_first), own, far, far_info
+    return (far_first, far_first), own, far, info, from_region(info), blocks
 
 
 def local(state, obs_pert, owners, loc_index, innov, obs_var, loc_scales):
     npatch = lax.axis_size("member")
-    info = pack(owners, loc_index, innov, obs_var, loc_scales)
-    orders, own, far, far_info = gather_rows(obs_pert[0], info, npatch)
+    facts = (owners, loc_index, innov, obs_var, loc_scales)
+    rows, width = state.shape
+    blocks = jnp.swapaxes(state.reshape(rows, npatch, width // npatch), 0, 1)
+    orders, own, far, info, far_info, blocks = gather_rows(obs_pert[0], facts, blocks, npatch)
     weights = solve(orders, own, far, info, far_info)
-    members = lax.all_to_all(state, "member", split_axis=1, concat_axis=0, tiled=True)
-    updated = update(weights, members)
+    members = lax.all_to_all(blocks, "member", split_axis=0, concat_axis=0, tiled=True)
+    updated = update(weights, members.reshape(rows * npatch, width // npatch))
     return lax.all_to_all(updated, "member", split_axis=0, concat_axis=1, tiled=True)
 
 

time: 80 us -> 77.6 us (0.970)
  waiting for transfers between devices: 11.8 us -> 10.7 us
  other arithmetic: 0.86 us -> 0.02 us
    reshape x0 -> x1, local copies, waits for them, and re-layouts: none -> 2.32 us  [local(): blocks = jnp.swapaxes(state.reshape(rows, npatch, width // npatch), 0, 1)]
    all_to_all x1 -> x0, local copies, waits for them, and re-layouts: 2.29 us -> none  [local(): lax.all_to_all(state, 'member', split_axis=1, concat_axis=0, tiled=True)]
    all_to_all x1, waiting for transfers between devices: 1.63 us -> 0.01 us  [local(): lax.all_to_all(blocks, 'member', split_axis=0, concat_axis=0, tiled=True)]
    concatenate x1, other arithmetic: 0.86 us -> 0.02 us  [gather_rows(): held = jnp.concatenate([shard] + got)]
    ppermute x6, waiting for transfers between devices: 9.86 us -> 10.7 us  [swap_by(): return lax.ppermute(block, ('region', 'member'), route)]
  transfers between devices with their start and end apart: 12 -> 12, of which waited for: 5 -> 5; matrix products, arithmetic and copies ran while one was open for 4% -> 3% of each run, Pallas kernels for 20% -> 21%
where the time goes in v4:
time: 77.6 us; the launch traced here: 77.3 us
  blocking collectives  30.3 us (39%)
  Pallas kernels  17.1 us (22%)
  starting transfers between devices  15.8 us (20%)
  waiting for transfers between devices  10.7 us (14%)
  local copies, waits for them, and re-layouts  3.38 us (4%)
    all_to_all x1, blocking collectives, local(): lax.all_to_all(updated, 'member', split_axis=0, concat_axis=1, tiled=True)  30.3 us
    pallas_call x1, Pallas kernels, solve(): pl.pallas_call(functools.partial(solve_kernel, orders, nparts), out_shape...  13.5 us
    ppermute x6, waiting for transfers between devices, swap_by(): return lax.ppermute(block, ('region', 'member'), route)  10.7 us
    ppermute x6, starting transfers between devices, swap_by(): return lax.ppermute(block, ('region', 'member'), route)  9.17 us
    all_to_all x1, starting transfers between devices, local(): lax.all_to_all(blocks, 'member', split_axis=0, concat_axis=0, tiled=True)  5.56 us
    reshape x1, local copies, waits for them, and re-layouts, local(): blocks = jnp.swapaxes(state.reshape(rows, npatch, width // npatch), 0, 1)  2.32 us
  transfers between devices with their start and end apart: 12, of which 5 were waited for; matrix products, arithmetic and copies ran while one was open for 3% of the time, Pallas kernels for 21%

profile of v4, /device:TPU:0, one launch (start us, length us, event | category | flops | bytes accessed | tf_op | source)
XLA Modules:
  0.0 77.3 jit_solution(16372245590539764752)
XLA Ops:
  0.0 5.0 %collective-permute-start.2 = (f32[32,512]{1,0:T(8,128)}, f32[32,512]{1,0:T(8,128)S(1)}, u32[]{:S(2)}, u32[]{:S(2)}) collective-permute-start(f32[32,512]{1,0:T(8,128)} %bitcast.17), channel_id=1, source_target_pairs={{0,12},{1,13},{2,14},{3,15},{4,8},{5,9},{6,10},{7,11},{8,4},{9,5},... | collective-permute-start | bytes 196616 | tf_op jit(solution)/shard_map/ppermute | solution.py:222
  5.0 0.0 collective-permute-start.1
  5.1 0.6 collective-permute-start
  5.6 0.0 copy-start.1
  5.6 2.3 %copy.13 = f32[4,16,8,512]{3,2,0,1:T(8,128)} copy(f32[4,16,8,512]{3,2,1,0:T(8,128)} %bitcast.16) | data formatting | bytes 2097152 | tf_op jit(solution)/shard_map/reshape | solution.py:256
  7.9 0.2 collective-permute-done.2
  8.2 1.8 %collective-permute-done.1 = f32[32,512]{1,0:T(8,128)S(1)} collective-permute-done((f32[32,512]{1,0:T(8,128)}, f32[32,512]{1,0:T(8,128)S(1)}, u32[]{:S(2)}, u32[]{:S(2)}) %collective-permute-start.1) | collective-permute-done | bytes 65568 | tf_op jit(solution)/shard_map/ppermute | solution.py:222
  9.9 1.0 %collective-permute-done = f32[32,512]{1,0:T(8,128)S(1)} collective-permute-done((f32[32,512]{1,0:T(8,128)}, f32[32,512]{1,0:T(8,128)S(1)}, u32[]{:S(2)}, u32[]{:S(2)}) %collective-permute-start) | collective-permute-done | bytes 65568 | tf_op jit(solution)/shard_map/ppermute | solution.py:222
  10.9 0.0 copy-done.1
  10.9 2.5 %collective-permute-start.8 = (f32[128,512]{1,0:T(8,128)S(1)}, f32[128,512]{1,0:T(8,128)S(1)}, u32[]{:S(2)}, u32[]{:S(2)}) collective-permute-start(f32[128,512]{1,0:T(8,128)S(1)} %pad_maximum_fusion.refs_0_), channel_id=1, source_target_pairs={{0,3},{1,2},{2,1},{3,0},{4,7},{5,6},{6,5},{7,4},{8,11},{9,10},{10,... | collective-permute-start | bytes 786440 | tf_op jit(solution)/shard_map/ppermute | solution.py:222
  13.4 0.5 collective-permute-start.6
  14.0 0.5 collective-permute-start.4
  14.5 1.4 %shard_map.73.refs_4_ = f32[8,512]{1,0:T(8,128)} custom-call(s32[1,512]{1,0:T(1,128)} %owner_ref, s32[1,512]{1,0:T(1,128)} %index_ref, f32[1,512]{1,0:T(1,128)} %innov_ref, f32[1,512]{1,0:T(1,128)} %var_ref, f32[8]{0:T(128)} %table_ref), custom_call_target="tpu_custom_call" | custom-call | tf_op jit(solution)/shard_map/pallas_call | solution.py:84
  15.9 0.0 copy-start
  15.9 5.6 %all-to-all-start = ((f32[16,32,512]{2,1,0:T(8,128)}), f32[16,32,512]{2,1,0:T(8,128)S(1)}, u32[]{:S(2)}, u32[]{:S(2)}) async-start(f32[16,32,512]{2,1,0:T(8,128)} %bitcast.12), calls=%async_computation | async-start | bytes 2097152 | tf_op jit(solution)/shard_map/all_to_all | solution.py:259
  21.5 0.1 collective-permute-start.3
  21.5 0.0 collective-permute-done.8.refs_3_
  21.5 0.5 collective-permute-start.9
  22.0 3.9 %collective-permute-done.6.refs_2_ = f32[128,512]{1,0:T(8,128)S(1)} collective-permute-done((f32[128,512]{1,0:T(8,128)S(1)}, f32[128,512]{1,0:T(8,128)S(1)}, u32[]{:S(2)}, u32[]{:S(2)}) %collective-permute-start.6) | collective-permute-done | bytes 262176 | tf_op jit(solution)/shard_map/ppermute | solution.py:222
  26.0 0.0 collective-permute-start.7
  26.0 3.8 %collective-permute-done.4.refs_1_ = f32[128,512]{1,0:T(8,128)S(1)} collective-permute-done((f32[128,512]{1,0:T(8,128)S(1)}, f32[128,512]{1,0:T(8,128)S(1)}, u32[]{:S(2)}, u32[]{:S(2)}) %collective-permute-start.4) | collective-permute-done | bytes 262176 | tf_op jit(solution)/shard_map/ppermute | solution.py:222
  29.8 0.0 collective-permute-start.5
  29.8 0.0 copy-done
  29.8 0.5 collective-permute-start.10
  30.3 1.0 %shard_map.74 = (f32[256,512]{1,0:T(8,128)S(1)}, f32[256,256]{1,0:T(8,128)S(1)}, f32[8,512]{1,0:T(8,128)S(1)}) custom-call(f32[128,512]{1,0:T(8,128)S(1)} %pad_maximum_fusion.refs_0_, f32[128,512]{1,0:T(8,128)S(1)} %collective-permute-done.4.refs_1_, f32[128,512]{1,0:T(8,128)S(1)} %collective-permute-done.6.refs_2_, ...), custom_call_target="tpu_custom_call" | custom-call | flops 805306368 | bytes 1048576 | tf_op jit(solution)/shard_map/pallas_call | solution.py:174
  31.3 0.0 collective-permute-done.10.refs_4_
  31.3 0.0 collective-permute-done.3.refs_0_
  31.3 0.0 collective-permute-done.9.refs_3_
  31.3 0.0 collective-permute-done.7.refs_2_
  31.4 0.0 collective-permute-done.5.refs_1_
  31.4 13.5 %shard_map.75.w_ref = bf16[2,512,512]{2,1,0:T(8,128)(2,1)S(1)} custom-call(f32[128,512]{1,0:T(8,128)S(1)} %collective-permute-done.3.refs_0_, f32[128,512]{1,0:T(8,128)S(1)} %collective-permute-done.5.refs_1_, f32[128,512]{1,0:T(8,128)S(1)} %collective-permute-done.7.refs_2_, f32[128,512]{1,0:T(8,128)S(1)} %collective-permute-done.9.refs_3_, ...), custom_call_target="tpu_custom_call" | custom-call | flops 16911433728 | bytes 1048576 | tf_op jit(solution)/shard_map/pallas_call | solution.py:185
  44.9 0.0 all-to-all-done
  44.9 1.1 %shard_map.76 = f32[512,512]{1,0:T(8,128)S(1)} custom-call(bf16[2,512,512]{2,1,0:T(8,128)(2,1)S(1)} %shard_map.75.w_ref, f32[512,512]{1,0:T(8,128)S(1)} %bitcast.13), custom_call_target="tpu_custom_call" | custom-call | flops 805306368 | bytes 3145728 | tf_op jit(solution)/shard_map/pallas_call | solution.py:207
  46.0 30.3 %all_to_all.24 = f32[16,32,512]{2,1,0:T(8,128)S(1)} all-to-all(f32[16,32,512]{2,1,0:T(8,128)S(1)} %bitcast.14), channel_id=1, replica_groups=mesh['region'=2,'member'=16] {'member'}, dimensions={0} | all-to-all | bytes 2097152 | tf_op jit(solution)/shard_map/all_to_all | solution.py:261
  76.3 1.1 %copy.11 = f32[16,4,8,512]{3,2,0,1:T(8,128)} copy(f32[16,4,8,512]{3,2,1,0:T(8,128)S(1)} %bitcast.15) | data formatting | bytes 2097152 | tf_op jit(solution)/shard_map/all_to_all | solution.py:261
  (1 shorter events, 0.0 us)
Async XLA Ops:
  0.0 8.2 %collective-permute-start.2 = (f32[32,512]{1,0:T(8,128)}, f32[32,512]{1,0:T(8,128)S(1)}, u32[]{:S(2)}, u32[]{:S(2)}) collective-permute-start(f32[32,512]{1,0:T(8,128)} %bitcast.17), channel_id=1, source_target_pairs={{0,12},{1,13},{2,14},{3,15},{4,8},{5,9},{6,10},{7,11},{8,4},{9,5},... | collective-permute-start | bytes 196616 | tf_op jit(solution)/shard_map/ppermute | solution.py:222
  5.0 4.9 %collective-permute-start.1 = (f32[32,512]{1,0:T(8,128)}, f32[32,512]{1,0:T(8,128)S(1)}, u32[]{:S(2)}, u32[]{:S(2)}) collective-permute-start(f32[32,512]{1,0:T(8,128)} %bitcast.18), channel_id=1, source_target_pairs={{0,4},{1,5},{2,6},{3,7},{4,0},{5,1},{6,2},{7,3},{8,12},{9,13},{10,... | collective-permute-start | bytes 196616 | tf_op jit(solution)/shard_map/ppermute | solution.py:222
  5.1 5.8 %collective-permute-start = (f32[32,512]{1,0:T(8,128)}, f32[32,512]{1,0:T(8,128)S(1)}, u32[]{:S(2)}, u32[]{:S(2)}) collective-permute-start(f32[32,512]{1,0:T(8,128)} %bitcast.19), channel_id=1, source_target_pairs={{0,8},{1,9},{2,10},{3,11},{4,12},{5,13},{6,14},{7,15},{8,0},{9,1},... | collective-permute-start | bytes 196616 | tf_op jit(solution)/shard_map/ppermute | solution.py:222
  5.6 5.3 %copy-start.1 = (f32[1,32,512]{2,1,0:T(8,128)S(1)}, f32[1,32,512]{2,1,0:T(8,128)}, u32[]{:S(2)}) copy-start(f32[1,32,512]{2,1,0:T(8,128)} %param.8) | copy-start | bytes 196612
  10.9 10.6 %collective-permute-start.8 = (f32[128,512]{1,0:T(8,128)S(1)}, f32[128,512]{1,0:T(8,128)S(1)}, u32[]{:S(2)}, u32[]{:S(2)}) collective-permute-start(f32[128,512]{1,0:T(8,128)S(1)} %pad_maximum_fusion.refs_0_), channel_id=1, source_target_pairs={{0,3},{1,2},{2,1},{3,0},{4,7},{5,6},{6,5},{7,4},{8,11},{9,10},{10,... | collective-permute-start | bytes 786440 | tf_op jit(solution)/shard_map/ppermute | solution.py:222
  13.4 12.5 %collective-permute-start.6 = (f32[128,512]{1,0:T(8,128)S(1)}, f32[128,512]{1,0:T(8,128)S(1)}, u32[]{:S(2)}, u32[]{:S(2)}) collective-permute-start(f32[128,512]{1,0:T(8,128)S(1)} %pad_maximum_fusion.refs_0_), channel_id=1, source_target_pairs={{0,1},{1,0},{2,3},{3,2},{4,5},{5,4},{6,7},{7,6},{8,9},{9,8},{10,11... | collective-permute-start | bytes 786440 | tf_op jit(solution)/shard_map/ppermute | solution.py:222
  14.0 15.8 %collective-permute-start.4 = (f32[128,512]{1,0:T(8,128)S(1)}, f32[128,512]{1,0:T(8,128)S(1)}, u32[]{:S(2)}, u32[]{:S(2)}) collective-permute-start(f32[128,512]{1,0:T(8,128)S(1)} %pad_maximum_fusion.refs_0_), channel_id=1, source_target_pairs={{0,2},{1,3},{2,0},{3,1},{4,6},{5,7},{6,4},{7,5},{8,10},{9,11},{10,... | collective-permute-start | bytes 786440 | tf_op jit(solution)/shard_map/ppermute | solution.py:222
  15.9 13.9 %copy-start = (f32[8,512]{1,0:T(8,128)S(1)}, f32[8,512]{1,0:T(8,128)}, u32[]{:S(2)}) copy-start(f32[8,512]{1,0:T(8,128)} %shard_map.73.refs_4_) | copy-start | bytes 49156
  15.9 29.0 %all-to-all-start = ((f32[16,32,512]{2,1,0:T(8,128)}), f32[16,32,512]{2,1,0:T(8,128)S(1)}, u32[]{:S(2)}, u32[]{:S(2)}) async-start(f32[16,32,512]{2,1,0:T(8,128)} %bitcast.12), calls=%async_computation | async-start | bytes 2097152 | tf_op jit(solution)/shard_map/all_to_all | solution.py:259
  21.5 9.9 %collective-permute-start.3 = (f32[128,512]{1,0:T(8,128)S(1)}, f32[128,512]{1,0:T(8,128)S(1)}, u32[]{:S(2)}, u32[]{:S(2)}) collective-permute-start(f32[128,512]{1,0:T(8,128)S(1)} %pad_maximum_fusion.refs_0_), channel_id=1, source_target_pairs={{0,16},{16,0},{1,17},{17,1},{2,18},{18,2},{3,19},{19,3},{4,20},{20... | collective-permute-start | bytes 786440 | tf_op jit(solution)/shard_map/ppermute | solution.py:229
  21.5 9.8 %collective-permute-start.9 = (f32[128,512]{1,0:T(8,128)S(1)}, f32[128,512]{1,0:T(8,128)S(1)}, u32[]{:S(2)}, u32[]{:S(2)}) collective-permute-start(f32[128,512]{1,0:T(8,128)S(1)} %collective-permute-done.8.refs_3_), channel_id=1, source_target_pairs={{0,16},{16,0},{1,17},{17,1},{2,18},{18,2},{3,19},{19,3},{4,20},{20... | collective-permute-start | bytes 786440 | tf_op jit(solution)/shard_map/ppermute | solution.py:229
  26.0 5.4 %collective-permute-start.7 = (f32[128,512]{1,0:T(8,128)S(1)}, f32[128,512]{1,0:T(8,128)S(1)}, u32[]{:S(2)}, u32[]{:S(2)}) collective-permute-start(f32[128,512]{1,0:T(8,128)S(1)} %collective-permute-done.6.refs_2_), channel_id=1, source_target_pairs={{0,16},{16,0},{1,17},{17,1},{2,18},{18,2},{3,19},{19,3},{4,20},{20... | collective-permute-start | bytes 786440 | tf_op jit(solution)/shard_map/ppermute | solution.py:229
  29.8 1.6 %collective-permute-start.5 = (f32[128,512]{1,0:T(8,128)S(1)}, f32[128,512]{1,0:T(8,128)S(1)}, u32[]{:S(2)}, u32[]{:S(2)}) collective-permute-start(f32[128,512]{1,0:T(8,128)S(1)} %collective-permute-done.4.refs_1_), channel_id=1, source_target_pairs={{0,16},{16,0},{1,17},{17,1},{2,18},{18,2},{3,19},{19,3},{4,20},{20... | collective-permute-start | bytes 786440 | tf_op jit(solution)/shard_map/ppermute | solution.py:229
  29.8 1.6 %collective-permute-start.10 = (f32[8,512]{1,0:T(8,128)S(1)}, f32[8,512]{1,0:T(8,128)S(1)}, u32[]{:S(2)}, u32[]{:S(2)}) collective-permute-start(f32[8,512]{1,0:T(8,128)S(1)} %copy-done), channel_id=1, source_target_pairs={{0,16},{16,0},{1,17},{17,1},{2,18},{18,2},{3,19},{19,3},{4,20},{20... | collective-permute-start | bytes 49160 | tf_op jit(solution)/shard_map/ppermute | solution.py:229

commit v5 on v4

--- a/solution.py
+++ b/solution.py
@@ -236,17 +236,19 @@
         same = list(range(whole.shape[0] // 32))
         info = pack(*facts)
         return (same, same), [whole], [from_region(whole)], info, from_region(info), blocks
-    far_steps = [2 * low, low, 3 * low]
-    near_steps = [2, 1, 3]
-    got = [swap_by(shard, count, a, b) for a, b in zip(far_steps, far_steps)]
+    far_steps = [(step * low, step * low) for step in (2, 1, 3)]
+    near_steps = [(2, 1), (1, 2), (3, 3)]
+    got = [swap_by(shard, count, a, b) for a, b in far_steps]
     held = jnp.concatenate([shard] + got)
     held, facts, blocks = lax.optimization_barrier((held, facts, blocks))
     info, blocks = lax.optimization_barrier((pack(*facts), blocks))
-    own = [held] + [swap_by(held, count, a, b) for a, b in zip(near_steps, near_steps)]
+    own = [held] + [swap_by(held, count, a, b) for a, b in near_steps]
     far = [from_region(part) for part in own]
-    far_first = [n ^ f for n in [0] + near_steps for f in [0] + far_steps]
-    near_first = [f ^ n for f in [0] + far_steps for n in [0] + near_steps]
-    return (far_first, far_first), own, far, info, from_region(info), blocks
+    orders = [
+        [n ^ f for n in [0] + [pair[r] for pair in near_steps] for f in [0] + [pair[r] for pair in far_steps]]
+        for r in (0, 1)
+    ]
+    return orders, own, far, info, from_region(info), blocks
 
 
 def local(state, obs_pert, owners, loc_index, innov, obs_var, loc_scales):

time: 77.6 us -> 77.6 us (level)
  no operation moved by 1% of the time
where the time goes in v5:
time: 77.6 us; the launch traced here: 77.3 us
  blocking collectives  30.2 us (39%)
  Pallas kernels  17.1 us (22%)
  starting transfers between devices  16.5 us (21%)
  waiting for transfers between devices  10.1 us (13%)
  local copies, waits for them, and re-layouts  3.38 us (4%)
    all_to_all x1, blocking collectives, local(): lax.all_to_all(updated, 'member', split_axis=0, concat_axis=1, tiled=True)  30.2 us
    pallas_call x1, Pallas kernels, solve(): pl.pallas_call(functools.partial(solve_kernel, orders, nparts), out_shape...  13.5 us
    ppermute x6, waiting for transfers between devices, swap_by(): return lax.ppermute(block, ('region', 'member'), route)  10 us
    ppermute x6, starting transfers between devices, swap_by(): return lax.ppermute(block, ('region', 'member'), route)  9.17 us
    all_to_all x1, starting transfers between devices, local(): lax.all_to_all(blocks, 'member', split_axis=0, concat_axis=0, tiled=True)  5.56 us
    reshape x1, local copies, waits for them, and re-layouts, local(): blocks = jnp.swapaxes(state.reshape(rows, npatch, width // npatch), 0, 1)  2.32 us
    ppermute x5, starting transfers between devices, from_region(): return lax.ppermute(block, 'region', REGIONS)  1.73 us
  transfers between devices with their start and end apart: 12, of which 5 were waited for; matrix products, arithmetic and copies ran while one was open for 3% of the time, Pallas kernels for 21%

profile of v5, /device:TPU:0, one launch (start us, length us, event | category | flops | bytes accessed | tf_op | source)
XLA Modules:
  0.0 77.3 jit_solution(10669497325465297730)
XLA Ops:
  0.0 5.0 %collective-permute-start.2 = (f32[32,512]{1,0:T(8,128)}, f32[32,512]{1,0:T(8,128)S(1)}, u32[]{:S(2)}, u32[]{:S(2)}) collective-permute-start(f32[32,512]{1,0:T(8,128)} %bitcast.17), channel_id=1, source_target_pairs={{0,12},{1,13},{2,14},{3,15},{4,8},{5,9},{6,10},{7,11},{8,4},{9,5},... | collective-permute-start | bytes 196616 | tf_op jit(solution)/shard_map/ppermute | solution.py:222
  5.0 0.0 collective-permute-start.1
  5.1 0.6 collective-permute-start
  5.6 0.0 copy-start.1
  5.6 2.3 %copy.13 = f32[4,16,8,512]{3,2,0,1:T(8,128)} copy(f32[4,16,8,512]{3,2,1,0:T(8,128)} %bitcast.16) | data formatting | bytes 2097152 | tf_op jit(solution)/shard_map/reshape | solution.py:258
  7.9 0.2 collective-permute-done.2
  8.2 1.8 %collective-permute-done.1 = f32[32,512]{1,0:T(8,128)S(1)} collective-permute-done((f32[32,512]{1,0:T(8,128)}, f32[32,512]{1,0:T(8,128)S(1)}, u32[]{:S(2)}, u32[]{:S(2)}) %collective-permute-start.1) | collective-permute-done | bytes 65568 | tf_op jit(solution)/shard_map/ppermute | solution.py:222
  9.9 1.0 %collective-permute-done = f32[32,512]{1,0:T(8,128)S(1)} collective-permute-done((f32[32,512]{1,0:T(8,128)}, f32[32,512]{1,0:T(8,128)S(1)}, u32[]{:S(2)}, u32[]{:S(2)}) %collective-permute-start) | collective-permute-done | bytes 65568 | tf_op jit(solution)/shard_map/ppermute | solution.py:222
  10.9 0.0 copy-done.1
  10.9 2.5 %collective-permute-start.8 = (f32[128,512]{1,0:T(8,128)S(1)}, f32[128,512]{1,0:T(8,128)S(1)}, u32[]{:S(2)}, u32[]{:S(2)}) collective-permute-start(f32[128,512]{1,0:T(8,128)S(1)} %pad_maximum_fusion.refs_0_), channel_id=1, source_target_pairs={{0,3},{1,2},{2,1},{3,0},{4,7},{5,6},{6,5},{7,4},{8,11},{9,10},{10,... | collective-permute-start | bytes 786440 | tf_op jit(solution)/shard_map/ppermute | solution.py:222
  13.4 0.5 collective-permute-start.6
  14.0 0.5 collective-permute-start.4
  14.5 1.4 %shard_map.73.refs_4_ = f32[8,512]{1,0:T(8,128)} custom-call(s32[1,512]{1,0:T(1,128)} %owner_ref, s32[1,512]{1,0:T(1,128)} %index_ref, f32[1,512]{1,0:T(1,128)} %innov_ref, f32[1,512]{1,0:T(1,128)} %var_ref, f32[8]{0:T(128)} %table_ref), custom_call_target="tpu_custom_call" | custom-call | tf_op jit(solution)/shard_map/pallas_call | solution.py:84
  15.9 0.0 copy-start
  15.9 5.6 %all-to-all-start = ((f32[16,32,512]{2,1,0:T(8,128)}), f32[16,32,512]{2,1,0:T(8,128)S(1)}, u32[]{:S(2)}, u32[]{:S(2)}) async-start(f32[16,32,512]{2,1,0:T(8,128)} %bitcast.12), calls=%async_computation | async-start | bytes 2097152 | tf_op jit(solution)/shard_map/all_to_all | solution.py:261
  21.5 0.1 collective-permute-start.3
  21.5 0.0 collective-permute-done.8.refs_3_
  21.5 0.5 collective-permute-start.9
  22.0 3.9 %collective-permute-done.6.refs_2_ = f32[128,512]{1,0:T(8,128)S(1)} collective-permute-done((f32[128,512]{1,0:T(8,128)S(1)}, f32[128,512]{1,0:T(8,128)S(1)}, u32[]{:S(2)}, u32[]{:S(2)}) %collective-permute-start.6) | collective-permute-done | bytes 262176 | tf_op jit(solution)/shard_map/ppermute | solution.py:222
  26.0 0.7 collective-permute-start.7
  26.6 3.1 %collective-permute-done.4.refs_1_ = f32[128,512]{1,0:T(8,128)S(1)} collective-permute-done((f32[128,512]{1,0:T(8,128)S(1)}, f32[128,512]{1,0:T(8,128)S(1)}, u32[]{:S(2)}, u32[]{:S(2)}) %collective-permute-start.4) | collective-permute-done | bytes 262176 | tf_op jit(solution)/shard_map/ppermute | solution.py:222
  29.8 0.0 collective-permute-start.5
  29.8 0.0 copy-done
  29.8 0.5 collective-permute-start.10
  30.3 1.0 %shard_map.74 = (f32[256,512]{1,0:T(8,128)S(1)}, f32[256,256]{1,0:T(8,128)S(1)}, f32[8,512]{1,0:T(8,128)S(1)}) custom-call(f32[128,512]{1,0:T(8,128)S(1)} %pad_maximum_fusion.refs_0_, f32[128,512]{1,0:T(8,128)S(1)} %collective-permute-done.4.refs_1_, f32[128,512]{1,0:T(8,128)S(1)} %collective-permute-done.6.refs_2_, ...), custom_call_target="tpu_custom_call" | custom-call | flops 805306368 | bytes 1048576 | tf_op jit(solution)/shard_map/pallas_call | solution.py:174
  31.3 0.0 collective-permute-done.10.refs_4_
  31.3 0.0 collective-permute-done.3.refs_0_
  31.3 0.0 collective-permute-done.9.refs_3_
  31.3 0.0 collective-permute-done.7.refs_2_
  31.4 0.0 collective-permute-done.5.refs_1_
  31.4 13.5 %shard_map.75.w_ref = bf16[2,512,512]{2,1,0:T(8,128)(2,1)S(1)} custom-call(f32[128,512]{1,0:T(8,128)S(1)} %collective-permute-done.3.refs_0_, f32[128,512]{1,0:T(8,128)S(1)} %collective-permute-done.5.refs_1_, f32[128,512]{1,0:T(8,128)S(1)} %collective-permute-done.7.refs_2_, f32[128,512]{1,0:T(8,128)S(1)} %collective-permute-done.9.refs_3_, ...), custom_call_target="tpu_custom_call" | custom-call | flops 16911433728 | bytes 1048576 | tf_op jit(solution)/shard_map/pallas_call | solution.py:185
  44.9 0.0 all-to-all-done
  44.9 1.1 %shard_map.76 = f32[512,512]{1,0:T(8,128)S(1)} custom-call(bf16[2,512,512]{2,1,0:T(8,128)(2,1)S(1)} %shard_map.75.w_ref, f32[512,512]{1,0:T(8,128)S(1)} %bitcast.13), custom_call_target="tpu_custom_call" | custom-call | flops 805306368 | bytes 3145728 | tf_op jit(solution)/shard_map/pallas_call | solution.py:207
  46.0 30.2 %all_to_all.24 = f32[16,32,512]{2,1,0:T(8,128)S(1)} all-to-all(f32[16,32,512]{2,1,0:T(8,128)S(1)} %bitcast.14), channel_id=1, replica_groups=mesh['region'=2,'member'=16] {'member'}, dimensions={0} | all-to-all | bytes 2097152 | tf_op jit(solution)/shard_map/all_to_all | solution.py:263
  76.2 1.1 %copy.11 = f32[16,4,8,512]{3,2,0,1:T(8,128)} copy(f32[16,4,8,512]{3,2,1,0:T(8,128)S(1)} %bitcast.15) | data formatting | bytes 2097152 | tf_op jit(solution)/shard_map/all_to_all | solution.py:263
  (1 shorter events, 0.0 us)
Async XLA Ops:
  0.0 8.2 %collective-permute-start.2 = (f32[32,512]{1,0:T(8,128)}, f32[32,512]{1,0:T(8,128)S(1)}, u32[]{:S(2)}, u32[]{:S(2)}) collective-permute-start(f32[32,512]{1,0:T(8,128)} %bitcast.17), channel_id=1, source_target_pairs={{0,12},{1,13},{2,14},{3,15},{4,8},{5,9},{6,10},{7,11},{8,4},{9,5},... | collective-permute-start | bytes 196616 | tf_op jit(solution)/shard_map/ppermute | solution.py:222
  5.0 4.9 %collective-permute-start.1 = (f32[32,512]{1,0:T(8,128)}, f32[32,512]{1,0:T(8,128)S(1)}, u32[]{:S(2)}, u32[]{:S(2)}) collective-permute-start(f32[32,512]{1,0:T(8,128)} %bitcast.18), channel_id=1, source_target_pairs={{0,4},{1,5},{2,6},{3,7},{4,0},{5,1},{6,2},{7,3},{8,12},{9,13},{10,... | collective-permute-start | bytes 196616 | tf_op jit(solution)/shard_map/ppermute | solution.py:222
  5.1 5.8 %collective-permute-start = (f32[32,512]{1,0:T(8,128)}, f32[32,512]{1,0:T(8,128)S(1)}, u32[]{:S(2)}, u32[]{:S(2)}) collective-permute-start(f32[32,512]{1,0:T(8,128)} %bitcast.19), channel_id=1, source_target_pairs={{0,8},{1,9},{2,10},{3,11},{4,12},{5,13},{6,14},{7,15},{8,0},{9,1},... | collective-permute-start | bytes 196616 | tf_op jit(solution)/shard_map/ppermute | solution.py:222
  5.6 5.3 %copy-start.1 = (f32[1,32,512]{2,1,0:T(8,128)S(1)}, f32[1,32,512]{2,1,0:T(8,128)}, u32[]{:S(2)}) copy-start(f32[1,32,512]{2,1,0:T(8,128)} %param.8) | copy-start | bytes 196612
  10.9 10.6 %collective-permute-start.8 = (f32[128,512]{1,0:T(8,128)S(1)}, f32[128,512]{1,0:T(8,128)S(1)}, u32[]{:S(2)}, u32[]{:S(2)}) collective-permute-start(f32[128,512]{1,0:T(8,128)S(1)} %pad_maximum_fusion.refs_0_), channel_id=1, source_target_pairs={{0,3},{1,2},{2,1},{3,0},{4,7},{5,6},{6,5},{7,4},{8,11},{9,10},{10,... | collective-permute-start | bytes 786440 | tf_op jit(solution)/shard_map/ppermute | solution.py:222
  13.4 12.5 %collective-permute-start.6 = (f32[128,512]{1,0:T(8,128)S(1)}, f32[128,512]{1,0:T(8,128)S(1)}, u32[]{:S(2)}, u32[]{:S(2)}) collective-permute-start(f32[128,512]{1,0:T(8,128)S(1)} %pad_maximum_fusion.refs_0_), channel_id=1, source_target_pairs={{0,1},{1,0},{2,3},{3,2},{4,5},{5,4},{6,7},{7,6},{8,9},{9,8},{10,11... | collective-permute-start | bytes 786440 | tf_op jit(solution)/shard_map/ppermute | solution.py:222
  14.0 15.8 %collective-permute-start.4 = (f32[128,512]{1,0:T(8,128)S(1)}, f32[128,512]{1,0:T(8,128)S(1)}, u32[]{:S(2)}, u32[]{:S(2)}) collective-permute-start(f32[128,512]{1,0:T(8,128)S(1)} %pad_maximum_fusion.refs_0_), channel_id=1, source_target_pairs={{0,2},{1,3},{2,0},{3,1},{4,6},{5,7},{6,4},{7,5},{8,10},{9,11},{10,... | collective-permute-start | bytes 786440 | tf_op jit(solution)/shard_map/ppermute | solution.py:222
  15.9 13.9 %copy-start = (f32[8,512]{1,0:T(8,128)S(1)}, f32[8,512]{1,0:T(8,128)}, u32[]{:S(2)}) copy-start(f32[8,512]{1,0:T(8,128)} %shard_map.73.refs_4_) | copy-start | bytes 49156
  15.9 29.0 %all-to-all-start = ((f32[16,32,512]{2,1,0:T(8,128)}), f32[16,32,512]{2,1,0:T(8,128)S(1)}, u32[]{:S(2)}, u32[]{:S(2)}) async-start(f32[16,32,512]{2,1,0:T(8,128)} %bitcast.12), calls=%async_computation | async-start | bytes 2097152 | tf_op jit(solution)/shard_map/all_to_all | solution.py:261
  21.5 9.9 %collective-permute-start.3 = (f32[128,512]{1,0:T(8,128)S(1)}, f32[128,512]{1,0:T(8,128)S(1)}, u32[]{:S(2)}, u32[]{:S(2)}) collective-permute-start(f32[128,512]{1,0:T(8,128)S(1)} %pad_maximum_fusion.refs_0_), channel_id=1, source_target_pairs={{0,16},{16,0},{1,17},{17,1},{2,18},{18,2},{3,19},{19,3},{4,20},{20... | collective-permute-start | bytes 786440 | tf_op jit(solution)/shard_map/ppermute | solution.py:229
  21.5 9.8 %collective-permute-start.9 = (f32[128,512]{1,0:T(8,128)S(1)}, f32[128,512]{1,0:T(8,128)S(1)}, u32[]{:S(2)}, u32[]{:S(2)}) collective-permute-start(f32[128,512]{1,0:T(8,128)S(1)} %collective-permute-done.8.refs_3_), channel_id=1, source_target_pairs={{0,16},{16,0},{1,17},{17,1},{2,18},{18,2},{3,19},{19,3},{4,20},{20... | collective-permute-start | bytes 786440 | tf_op jit(solution)/shard_map/ppermute | solution.py:229
  26.0 5.4 %collective-permute-start.7 = (f32[128,512]{1,0:T(8,128)S(1)}, f32[128,512]{1,0:T(8,128)S(1)}, u32[]{:S(2)}, u32[]{:S(2)}) collective-permute-start(f32[128,512]{1,0:T(8,128)S(1)} %collective-permute-done.6.refs_2_), channel_id=1, source_target_pairs={{0,16},{16,0},{1,17},{17,1},{2,18},{18,2},{3,19},{19,3},{4,20},{20... | collective-permute-start | bytes 786440 | tf_op jit(solution)/shard_map/ppermute | solution.py:229
  29.8 1.6 %collective-permute-start.5 = (f32[128,512]{1,0:T(8,128)S(1)}, f32[128,512]{1,0:T(8,128)S(1)}, u32[]{:S(2)}, u32[]{:S(2)}) collective-permute-start(f32[128,512]{1,0:T(8,128)S(1)} %collective-permute-done.4.refs_1_), channel_id=1, source_target_pairs={{0,16},{16,0},{1,17},{17,1},{2,18},{18,2},{3,19},{19,3},{4,20},{20... | collective-permute-start | bytes 786440 | tf_op jit(solution)/shard_map/ppermute | solution.py:229
  29.8 1.6 %collective-permute-start.10 = (f32[8,512]{1,0:T(8,128)S(1)}, f32[8,512]{1,0:T(8,128)S(1)}, u32[]{:S(2)}, u32[]{:S(2)}) collective-permute-start(f32[8,512]{1,0:T(8,128)S(1)} %copy-done), channel_id=1, source_target_pairs={{0,16},{16,0},{1,17},{17,1},{2,18},{18,2},{3,19},{19,3},{4,20},{20... | collective-permute-start | bytes 49160 | tf_op jit(solution)/shard_map/ppermute | solution.py:229

commit v6 on v4

--- a/solution.py
+++ b/solution.py
@@ -61,9 +61,10 @@
 
 def sym_put(ref, top, low, half):
     first, rest = slice(0, half), slice(half, None)
-    put_at(ref, first, slice(None), top)
+    for i, part in enumerate(split(top)):
+        ref[i, first, :] = part
+        ref[i, rest, first] = part[:, half:].T
     put_at(ref, rest, rest, low)
-    put_at(ref, rest, first, top[:, half:].T)
 
 
 def pack_kernel(owner_ref, index_ref, innov_ref, var_ref, table_ref, o_ref):

time: 77.6 us -> 77.5 us (level)
  transfers between devices with their start and end apart: 12 -> 12, of which waited for: 5 -> 5; matrix products, arithmetic and copies ran while one was open for 3% -> 3% of each run, Pallas kernels for 21% -> 20%
where the time goes in v6:
time: 77.5 us; the launch traced here: 77.2 us
  blocking collectives  30.3 us (39%)
  Pallas kernels  16.9 us (22%)
  starting transfers between devices  15.8 us (20%)
  waiting for transfers between devices  10.7 us (14%)
  local copies, waits for them, and re-layouts  3.38 us (4%)
    all_to_all x1, blocking collectives, local(): lax.all_to_all(updated, 'member', split_axis=0, concat_axis=1, tiled=True)  30.3 us
    pallas_call x1, Pallas kernels, solve(): pl.pallas_call(functools.partial(solve_kernel, orders, nparts), out_shape...  13.3 us
    ppermute x6, waiting for transfers between devices, swap_by(): return lax.ppermute(block, ('region', 'member'), route)  10.7 us
    ppermute x6, starting transfers between devices, swap_by(): return lax.ppermute(block, ('region', 'member'), route)  9.17 us
    all_to_all x1, starting transfers between devices, local(): lax.all_to_all(blocks, 'member', split_axis=0, concat_axis=0, tiled=True)  5.56 us
    reshape x1, local copies, waits for them, and re-layouts, local(): blocks = jnp.swapaxes(state.reshape(rows, npatch, width // npatch), 0, 1)  2.32 us
  transfers between devices with their start and end apart: 12, of which 5 were waited for; matrix products, arithmetic and copies ran while one was open for 3% of the time, Pallas kernels for 20%

profile of v6, /device:TPU:0, one launch (start us, length us, event | category | flops | bytes accessed | tf_op | source)
XLA Modules:
  0.0 77.2 jit_solution(3280169758887676101)
XLA Ops:
  0.0 5.0 %collective-permute-start.2 = (f32[32,512]{1,0:T(8,128)}, f32[32,512]{1,0:T(8,128)S(1)}, u32[]{:S(2)}, u32[]{:S(2)}) collective-permute-start(f32[32,512]{1,0:T(8,128)} %bitcast.17), channel_id=1, source_target_pairs={{0,12},{1,13},{2,14},{3,15},{4,8},{5,9},{6,10},{7,11},{8,4},{9,5},... | collective-permute-start | bytes 196616 | tf_op jit(solution)/shard_map/ppermute | solution.py:223
  5.0 0.0 collective-permute-start.1
  5.1 0.6 collective-permute-start
  5.6 0.0 copy-start.1
  5.6 2.3 %copy.13 = f32[4,16,8,512]{3,2,0,1:T(8,128)} copy(f32[4,16,8,512]{3,2,1,0:T(8,128)} %bitcast.16) | data formatting | bytes 2097152 | tf_op jit(solution)/shard_map/reshape | solution.py:257
  7.9 0.2 collective-permute-done.2
  8.2 1.8 %collective-permute-done.1 = f32[32,512]{1,0:T(8,128)S(1)} collective-permute-done((f32[32,512]{1,0:T(8,128)}, f32[32,512]{1,0:T(8,128)S(1)}, u32[]{:S(2)}, u32[]{:S(2)}) %collective-permute-start.1) | collective-permute-done | bytes 65568 | tf_op jit(solution)/shard_map/ppermute | solution.py:223
  9.9 1.0 %collective-permute-done = f32[32,512]{1,0:T(8,128)S(1)} collective-permute-done((f32[32,512]{1,0:T(8,128)}, f32[32,512]{1,0:T(8,128)S(1)}, u32[]{:S(2)}, u32[]{:S(2)}) %collective-permute-start) | collective-permute-done | bytes 65568 | tf_op jit(solution)/shard_map/ppermute | solution.py:223
  10.9 0.0 copy-done.1
  10.9 2.5 %collective-permute-start.8 = (f32[128,512]{1,0:T(8,128)S(1)}, f32[128,512]{1,0:T(8,128)S(1)}, u32[]{:S(2)}, u32[]{:S(2)}) collective-permute-start(f32[128,512]{1,0:T(8,128)S(1)} %pad_maximum_fusion.refs_0_), channel_id=1, source_target_pairs={{0,3},{1,2},{2,1},{3,0},{4,7},{5,6},{6,5},{7,4},{8,11},{9,10},{10,... | collective-permute-start | bytes 786440 | tf_op jit(solution)/shard_map/ppermute | solution.py:223
  13.4 0.5 collective-permute-start.6
  14.0 0.5 collective-permute-start.4
  14.5 1.4 %shard_map.73.refs_4_ = f32[8,512]{1,0:T(8,128)} custom-call(s32[1,512]{1,0:T(1,128)} %owner_ref, s32[1,512]{1,0:T(1,128)} %index_ref, f32[1,512]{1,0:T(1,128)} %innov_ref, f32[1,512]{1,0:T(1,128)} %var_ref, f32[8]{0:T(128)} %table_ref), custom_call_target="tpu_custom_call" | custom-call | tf_op jit(solution)/shard_map/pallas_call | solution.py:85
  15.9 0.0 copy-start
  15.9 5.6 %all-to-all-start = ((f32[16,32,512]{2,1,0:T(8,128)}), f32[16,32,512]{2,1,0:T(8,128)S(1)}, u32[]{:S(2)}, u32[]{:S(2)}) async-start(f32[16,32,512]{2,1,0:T(8,128)} %bitcast.12), calls=%async_computation | async-start | bytes 2097152 | tf_op jit(solution)/shard_map/all_to_all | solution.py:260
  21.5 0.1 collective-permute-start.3
  21.5 0.0 collective-permute-done.8.refs_3_
  21.5 0.5 collective-permute-start.9
  22.0 3.9 %collective-permute-done.6.refs_2_ = f32[128,512]{1,0:T(8,128)S(1)} collective-permute-done((f32[128,512]{1,0:T(8,128)S(1)}, f32[128,512]{1,0:T(8,128)S(1)}, u32[]{:S(2)}, u32[]{:S(2)}) %collective-permute-start.6) | collective-permute-done | bytes 262176 | tf_op jit(solution)/shard_map/ppermute | solution.py:223
  26.0 0.0 collective-permute-start.7
  26.0 3.8 %collective-permute-done.4.refs_1_ = f32[128,512]{1,0:T(8,128)S(1)} collective-permute-done((f32[128,512]{1,0:T(8,128)S(1)}, f32[128,512]{1,0:T(8,128)S(1)}, u32[]{:S(2)}, u32[]{:S(2)}) %collective-permute-start.4) | collective-permute-done | bytes 262176 | tf_op jit(solution)/shard_map/ppermute | solution.py:223
  29.8 0.0 collective-permute-start.5
  29.8 0.0 copy-done
  29.8 0.5 collective-permute-start.10
  30.3 1.0 %shard_map.74 = (f32[256,512]{1,0:T(8,128)S(1)}, f32[256,256]{1,0:T(8,128)S(1)}, f32[8,512]{1,0:T(8,128)S(1)}) custom-call(f32[128,512]{1,0:T(8,128)S(1)} %pad_maximum_fusion.refs_0_, f32[128,512]{1,0:T(8,128)S(1)} %collective-permute-done.4.refs_1_, f32[128,512]{1,0:T(8,128)S(1)} %collective-permute-done.6.refs_2_, ...), custom_call_target="tpu_custom_call" | custom-call | flops 805306368 | bytes 1048576 | tf_op jit(solution)/shard_map/pallas_call | solution.py:175
  31.3 0.0 collective-permute-done.10.refs_4_
  31.3 0.0 collective-permute-done.3.refs_0_
  31.3 0.0 collective-permute-done.9.refs_3_
  31.3 0.0 collective-permute-done.7.refs_2_
  31.4 0.0 collective-permute-done.5.refs_1_
  31.4 13.3 %shard_map.75.w_ref = bf16[2,512,512]{2,1,0:T(8,128)(2,1)S(1)} custom-call(f32[128,512]{1,0:T(8,128)S(1)} %collective-permute-done.3.refs_0_, f32[128,512]{1,0:T(8,128)S(1)} %collective-permute-done.5.refs_1_, f32[128,512]{1,0:T(8,128)S(1)} %collective-permute-done.7.refs_2_, f32[128,512]{1,0:T(8,128)S(1)} %collective-permute-done.9.refs_3_, ...), custom_call_target="tpu_custom_call" | custom-call | flops 16911433728 | bytes 1048576 | tf_op jit(solution)/shard_map/pallas_call | solution.py:186
  44.7 0.0 all-to-all-done
  44.7 1.1 %shard_map.76 = f32[512,512]{1,0:T(8,128)S(1)} custom-call(bf16[2,512,512]{2,1,0:T(8,128)(2,1)S(1)} %shard_map.75.w_ref, f32[512,512]{1,0:T(8,128)S(1)} %bitcast.13), custom_call_target="tpu_custom_call" | custom-call | flops 805306368 | bytes 3145728 | tf_op jit(solution)/shard_map/pallas_call | solution.py:208
  45.8 30.3 %all_to_all.24 = f32[16,32,512]{2,1,0:T(8,128)S(1)} all-to-all(f32[16,32,512]{2,1,0:T(8,128)S(1)} %bitcast.14), channel_id=1, replica_groups=mesh['region'=2,'member'=16] {'member'}, dimensions={0} | all-to-all | bytes 2097152 | tf_op jit(solution)/shard_map/all_to_all | solution.py:262
  76.1 1.1 %copy.11 = f32[16,4,8,512]{3,2,0,1:T(8,128)} copy(f32[16,4,8,512]{3,2,1,0:T(8,128)S(1)} %bitcast.15) | data formatting | bytes 2097152 | tf_op jit(solution)/shard_map/all_to_all | solution.py:262
  (1 shorter events, 0.0 us)
Async XLA Ops:
  0.0 8.2 %collective-permute-start.2 = (f32[32,512]{1,0:T(8,128)}, f32[32,512]{1,0:T(8,128)S(1)}, u32[]{:S(2)}, u32[]{:S(2)}) collective-permute-start(f32[32,512]{1,0:T(8,128)} %bitcast.17), channel_id=1, source_target_pairs={{0,12},{1,13},{2,14},{3,15},{4,8},{5,9},{6,10},{7,11},{8,4},{9,5},... | collective-permute-start | bytes 196616 | tf_op jit(solution)/shard_map/ppermute | solution.py:223
  5.0 4.9 %collective-permute-start.1 = (f32[32,512]{1,0:T(8,128)}, f32[32,512]{1,0:T(8,128)S(1)}, u32[]{:S(2)}, u32[]{:S(2)}) collective-permute-start(f32[32,512]{1,0:T(8,128)} %bitcast.18), channel_id=1, source_target_pairs={{0,4},{1,5},{2,6},{3,7},{4,0},{5,1},{6,2},{7,3},{8,12},{9,13},{10,... | collective-permute-start | bytes 196616 | tf_op jit(solution)/shard_map/ppermute | solution.py:223
  5.1 5.8 %collective-permute-start = (f32[32,512]{1,0:T(8,128)}, f32[32,512]{1,0:T(8,128)S(1)}, u32[]{:S(2)}, u32[]{:S(2)}) collective-permute-start(f32[32,512]{1,0:T(8,128)} %bitcast.19), channel_id=1, source_target_pairs={{0,8},{1,9},{2,10},{3,11},{4,12},{5,13},{6,14},{7,15},{8,0},{9,1},... | collective-permute-start | bytes 196616 | tf_op jit(solution)/shard_map/ppermute | solution.py:223
  5.6 5.3 %copy-start.1 = (f32[1,32,512]{2,1,0:T(8,128)S(1)}, f32[1,32,512]{2,1,0:T(8,128)}, u32[]{:S(2)}) copy-start(f32[1,32,512]{2,1,0:T(8,128)} %param.8) | copy-start | bytes 196612
  10.9 10.6 %collective-permute-start.8 = (f32[128,512]{1,0:T(8,128)S(1)}, f32[128,512]{1,0:T(8,128)S(1)}, u32[]{:S(2)}, u32[]{:S(2)}) collective-permute-start(f32[128,512]{1,0:T(8,128)S(1)} %pad_maximum_fusion.refs_0_), channel_id=1, source_target_pairs={{0,3},{1,2},{2,1},{3,0},{4,7},{5,6},{6,5},{7,4},{8,11},{9,10},{10,... | collective-permute-start | bytes 786440 | tf_op jit(solution)/shard_map/ppermute | solution.py:223
  13.4 12.5 %collective-permute-start.6 = (f32[128,512]{1,0:T(8,128)S(1)}, f32[128,512]{1,0:T(8,128)S(1)}, u32[]{:S(2)}, u32[]{:S(2)}) collective-permute-start(f32[128,512]{1,0:T(8,128)S(1)} %pad_maximum_fusion.refs_0_), channel_id=1, source_target_pairs={{0,1},{1,0},{2,3},{3,2},{4,5},{5,4},{6,7},{7,6},{8,9},{9,8},{10,11... | collective-permute-start | bytes 786440 | tf_op jit(solution)/shard_map/ppermute | solution.py:223
  14.0 15.8 %collective-permute-start.4 = (f32[128,512]{1,0:T(8,128)S(1)}, f32[128,512]{1,0:T(8,128)S(1)}, u32[]{:S(2)}, u32[]{:S(2)}) collective-permute-start(f32[128,512]{1,0:T(8,128)S(1)} %pad_maximum_fusion.refs_0_), channel_id=1, source_target_pairs={{0,2},{1,3},{2,0},{3,1},{4,6},{5,7},{6,4},{7,5},{8,10},{9,11},{10,... | collective-permute-start | bytes 786440 | tf_op jit(solution)/shard_map/ppermute | solution.py:223
  15.9 13.9 %copy-start = (f32[8,512]{1,0:T(8,128)S(1)}, f32[8,512]{1,0:T(8,128)}, u32[]{:S(2)}) copy-start(f32[8,512]{1,0:T(8,128)} %shard_map.73.refs_4_) | copy-start | bytes 49156
  15.9 28.8 %all-to-all-start = ((f32[16,32,512]{2,1,0:T(8,128)}), f32[16,32,512]{2,1,0:T(8,128)S(1)}, u32[]{:S(2)}, u32[]{:S(2)}) async-start(f32[16,32,512]{2,1,0:T(8,128)} %bitcast.12), calls=%async_computation | async-start | bytes 2097152 | tf_op jit(solution)/shard_map/all_to_all | solution.py:260
  21.5 9.9 %collective-permute-start.3 = (f32[128,512]{1,0:T(8,128)S(1)}, f32[128,512]{1,0:T(8,128)S(1)}, u32[]{:S(2)}, u32[]{:S(2)}) collective-permute-start(f32[128,512]{1,0:T(8,128)S(1)} %pad_maximum_fusion.refs_0_), channel_id=1, source_target_pairs={{0,16},{16,0},{1,17},{17,1},{2,18},{18,2},{3,19},{19,3},{4,20},{20... | collective-permute-start | bytes 786440 | tf_op jit(solution)/shard_map/ppermute | solution.py:230
  21.5 9.8 %collective-permute-start.9 = (f32[128,512]{1,0:T(8,128)S(1)}, f32[128,512]{1,0:T(8,128)S(1)}, u32[]{:S(2)}, u32[]{:S(2)}) collective-permute-start(f32[128,512]{1,0:T(8,128)S(1)} %collective-permute-done.8.refs_3_), channel_id=1, source_target_pairs={{0,16},{16,0},{1,17},{17,1},{2,18},{18,2},{3,19},{19,3},{4,20},{20... | collective-permute-start | bytes 786440 | tf_op jit(solution)/shard_map/ppermute | solution.py:230
  26.0 5.4 %collective-permute-start.7 = (f32[128,512]{1,0:T(8,128)S(1)}, f32[128,512]{1,0:T(8,128)S(1)}, u32[]{:S(2)}, u32[]{:S(2)}) collective-permute-start(f32[128,512]{1,0:T(8,128)S(1)} %collective-permute-done.6.refs_2_), channel_id=1, source_target_pairs={{0,16},{16,0},{1,17},{17,1},{2,18},{18,2},{3,19},{19,3},{4,20},{20... | collective-permute-start | bytes 786440 | tf_op jit(solution)/shard_map/ppermute | solution.py:230
  29.8 1.6 %collective-permute-start.5 = (f32[128,512]{1,0:T(8,128)S(1)}, f32[128,512]{1,0:T(8,128)S(1)}, u32[]{:S(2)}, u32[]{:S(2)}) collective-permute-start(f32[128,512]{1,0:T(8,128)S(1)} %collective-permute-done.4.refs_1_), channel_id=1, source_target_pairs={{0,16},{16,0},{1,17},{17,1},{2,18},{18,2},{3,19},{19,3},{4,20},{20... | collective-permute-start | bytes 786440 | tf_op jit(solution)/shard_map/ppermute | solution.py:230
  29.8 1.6 %collective-permute-start.10 = (f32[8,512]{1,0:T(8,128)S(1)}, f32[8,512]{1,0:T(8,128)S(1)}, u32[]{:S(2)}, u32[]{:S(2)}) collective-permute-start(f32[8,512]{1,0:T(8,128)S(1)} %copy-done), channel_id=1, source_target_pairs={{0,16},{16,0},{1,17},{17,1},{2,18},{18,2},{3,19},{19,3},{4,20},{20... | collective-permute-start | bytes 49160 | tf_op jit(solution)/shard_map/ppermute | solution.py:230

commit v7 on v5

--- a/solution.py
+++ b/solution.py
@@ -61,9 +61,10 @@
 
 def sym_put(ref, top, low, half):
     first, rest = slice(0, half), slice(half, None)
-    put_at(ref, first, slice(None), top)
+    for i, part in enumerate(split(top)):
+        ref[i, first, :] = part
+        ref[i, rest, first] = part[:, half:].T
     put_at(ref, rest, rest, low)
-    put_at(ref, rest, first, top[:, half:].T)
 
 
 def pack_kernel(owner_ref, index_ref, innov_ref, var_ref, table_ref, o_ref):

time: 77.6 us -> 77.5 us (level)
  transfers between devices with their start and end apart: 12 -> 12, of which waited for: 5 -> 5; matrix products, arithmetic and copies ran while one was open for 3% -> 3% of each run, Pallas kernels for 21% -> 20%
where the time goes in v7:
time: 77.5 us; the launch traced here: 77.2 us
  blocking collectives  30.3 us (39%)
  Pallas kernels  16.9 us (22%)
  starting transfers between devices  16.5 us (21%)
  waiting for transfers between devices  10.1 us (13%)
  local copies, waits for them, and re-layouts  3.38 us (4%)
    all_to_all x1, blocking collectives, local(): lax.all_to_all(updated, 'member', split_axis=0, concat_axis=1, tiled=True)  30.3 us
    pallas_call x1, Pallas kernels, solve(): pl.pallas_call(functools.partial(solve_kernel, orders, nparts), out_shape...  13.3 us
    ppermute x6, waiting for transfers between devices, swap_by(): return lax.ppermute(block, ('region', 'member'), route)  10 us
    ppermute x6, starting transfers between devices, swap_by(): return lax.ppermute(block, ('region', 'member'), route)  9.17 us
    all_to_all x1, starting transfers between devices, local(): lax.all_to_all(blocks, 'member', split_axis=0, concat_axis=0, tiled=True)  5.56 us
    reshape x1, local copies, waits for them, and re-layouts, local(): blocks = jnp.swapaxes(state.reshape(rows, npatch, width // npatch), 0, 1)  2.32 us
    ppermute x5, starting transfers between devices, from_region(): return lax.ppermute(block, 'region', REGIONS)  1.73 us
  transfers between devices with their start and end apart: 12, of which 5 were waited for; matrix products, arithmetic and copies ran while one was open for 3% of the time, Pallas kernels for 20%

profile of v7, /device:TPU:0, one launch (start us, length us, event | category | flops | bytes accessed | tf_op | source)
XLA Modules:
  0.0 77.2 jit_solution(9567398646411265907)
XLA Ops:
  0.0 5.0 %collective-permute-start.2 = (f32[32,512]{1,0:T(8,128)}, f32[32,512]{1,0:T(8,128)S(1)}, u32[]{:S(2)}, u32[]{:S(2)}) collective-permute-start(f32[32,512]{1,0:T(8,128)} %bitcast.17), channel_id=1, source_target_pairs={{0,12},{1,13},{2,14},{3,15},{4,8},{5,9},{6,10},{7,11},{8,4},{9,5},... | collective-permute-start | bytes 196616 | tf_op jit(solution)/shard_map/ppermute | solution.py:223
  5.0 0.0 collective-permute-start.1
  5.1 0.6 collective-permute-start
  5.6 0.0 copy-start.1
  5.6 2.3 %copy.13 = f32[4,16,8,512]{3,2,0,1:T(8,128)} copy(f32[4,16,8,512]{3,2,1,0:T(8,128)} %bitcast.16) | data formatting | bytes 2097152 | tf_op jit(solution)/shard_map/reshape | solution.py:259
  7.9 0.2 collective-permute-done.2
  8.2 1.8 %collective-permute-done.1 = f32[32,512]{1,0:T(8,128)S(1)} collective-permute-done((f32[32,512]{1,0:T(8,128)}, f32[32,512]{1,0:T(8,128)S(1)}, u32[]{:S(2)}, u32[]{:S(2)}) %collective-permute-start.1) | collective-permute-done | bytes 65568 | tf_op jit(solution)/shard_map/ppermute | solution.py:223
  9.9 1.0 %collective-permute-done = f32[32,512]{1,0:T(8,128)S(1)} collective-permute-done((f32[32,512]{1,0:T(8,128)}, f32[32,512]{1,0:T(8,128)S(1)}, u32[]{:S(2)}, u32[]{:S(2)}) %collective-permute-start) | collective-permute-done | bytes 65568 | tf_op jit(solution)/shard_map/ppermute | solution.py:223
  10.9 0.0 copy-done.1
  10.9 2.5 %collective-permute-start.8 = (f32[128,512]{1,0:T(8,128)S(1)}, f32[128,512]{1,0:T(8,128)S(1)}, u32[]{:S(2)}, u32[]{:S(2)}) collective-permute-start(f32[128,512]{1,0:T(8,128)S(1)} %pad_maximum_fusion.refs_0_), channel_id=1, source_target_pairs={{0,3},{1,2},{2,1},{3,0},{4,7},{5,6},{6,5},{7,4},{8,11},{9,10},{10,... | collective-permute-start | bytes 786440 | tf_op jit(solution)/shard_map/ppermute | solution.py:223
  13.4 0.5 collective-permute-start.6
  14.0 0.5 collective-permute-start.4
  14.5 1.4 %shard_map.73.refs_4_ = f32[8,512]{1,0:T(8,128)} custom-call(s32[1,512]{1,0:T(1,128)} %owner_ref, s32[1,512]{1,0:T(1,128)} %index_ref, f32[1,512]{1,0:T(1,128)} %innov_ref, f32[1,512]{1,0:T(1,128)} %var_ref, f32[8]{0:T(128)} %table_ref), custom_call_target="tpu_custom_call" | custom-call | tf_op jit(solution)/shard_map/pallas_call | solution.py:85
  15.9 0.0 copy-start
  15.9 5.6 %all-to-all-start = ((f32[16,32,512]{2,1,0:T(8,128)}), f32[16,32,512]{2,1,0:T(8,128)S(1)}, u32[]{:S(2)}, u32[]{:S(2)}) async-start(f32[16,32,512]{2,1,0:T(8,128)} %bitcast.12), calls=%async_computation | async-start | bytes 2097152 | tf_op jit(solution)/shard_map/all_to_all | solution.py:262
  21.5 0.1 collective-permute-start.3
  21.5 0.0 collective-permute-done.8.refs_3_
  21.5 0.5 collective-permute-start.9
  22.0 3.9 %collective-permute-done.6.refs_2_ = f32[128,512]{1,0:T(8,128)S(1)} collective-permute-done((f32[128,512]{1,0:T(8,128)S(1)}, f32[128,512]{1,0:T(8,128)S(1)}, u32[]{:S(2)}, u32[]{:S(2)}) %collective-permute-start.6) | collective-permute-done | bytes 262176 | tf_op jit(solution)/shard_map/ppermute | solution.py:223
  26.0 0.7 collective-permute-start.7
  26.6 3.1 %collective-permute-done.4.refs_1_ = f32[128,512]{1,0:T(8,128)S(1)} collective-permute-done((f32[128,512]{1,0:T(8,128)S(1)}, f32[128,512]{1,0:T(8,128)S(1)}, u32[]{:S(2)}, u32[]{:S(2)}) %collective-permute-start.4) | collective-permute-done | bytes 262176 | tf_op jit(solution)/shard_map/ppermute | solution.py:223
  29.8 0.0 collective-permute-start.5
  29.8 0.0 copy-done
  29.8 0.5 collective-permute-start.10
  30.3 1.0 %shard_map.74 = (f32[256,512]{1,0:T(8,128)S(1)}, f32[256,256]{1,0:T(8,128)S(1)}, f32[8,512]{1,0:T(8,128)S(1)}) custom-call(f32[128,512]{1,0:T(8,128)S(1)} %pad_maximum_fusion.refs_0_, f32[128,512]{1,0:T(8,128)S(1)} %collective-permute-done.4.refs_1_, f32[128,512]{1,0:T(8,128)S(1)} %collective-permute-done.6.refs_2_, ...), custom_call_target="tpu_custom_call" | custom-call | flops 805306368 | bytes 1048576 | tf_op jit(solution)/shard_map/pallas_call | solution.py:175
  31.3 0.0 collective-permute-done.10.refs_4_
  31.3 0.0 collective-permute-done.3.refs_0_
  31.3 0.0 collective-permute-done.9.refs_3_
  31.3 0.0 collective-permute-done.7.refs_2_
  31.4 0.0 collective-permute-done.5.refs_1_
  31.4 13.3 %shard_map.75.w_ref = bf16[2,512,512]{2,1,0:T(8,128)(2,1)S(1)} custom-call(f32[128,512]{1,0:T(8,128)S(1)} %collective-permute-done.3.refs_0_, f32[128,512]{1,0:T(8,128)S(1)} %collective-permute-done.5.refs_1_, f32[128,512]{1,0:T(8,128)S(1)} %collective-permute-done.7.refs_2_, f32[128,512]{1,0:T(8,128)S(1)} %collective-permute-done.9.refs_3_, ...), custom_call_target="tpu_custom_call" | custom-call | flops 16911433728 | bytes 1048576 | tf_op jit(solution)/shard_map/pallas_call | solution.py:186
  44.7 0.0 all-to-all-done
  44.7 1.1 %shard_map.76 = f32[512,512]{1,0:T(8,128)S(1)} custom-call(bf16[2,512,512]{2,1,0:T(8,128)(2,1)S(1)} %shard_map.75.w_ref, f32[512,512]{1,0:T(8,128)S(1)} %bitcast.13), custom_call_target="tpu_custom_call" | custom-call | flops 805306368 | bytes 3145728 | tf_op jit(solution)/shard_map/pallas_call | solution.py:208
  45.8 30.3 %all_to_all.24 = f32[16,32,512]{2,1,0:T(8,128)S(1)} all-to-all(f32[16,32,512]{2,1,0:T(8,128)S(1)} %bitcast.14), channel_id=1, replica_groups=mesh['region'=2,'member'=16] {'member'}, dimensions={0} | all-to-all | bytes 2097152 | tf_op jit(solution)/shard_map/all_to_all | solution.py:264
  76.1 1.1 %copy.11 = f32[16,4,8,512]{3,2,0,1:T(8,128)} copy(f32[16,4,8,512]{3,2,1,0:T(8,128)S(1)} %bitcast.15) | data formatting | bytes 2097152 | tf_op jit(solution)/shard_map/all_to_all | solution.py:264
  (1 shorter events, 0.0 us)
Async XLA Ops:
  0.0 8.2 %collective-permute-start.2 = (f32[32,512]{1,0:T(8,128)}, f32[32,512]{1,0:T(8,128)S(1)}, u32[]{:S(2)}, u32[]{:S(2)}) collective-permute-start(f32[32,512]{1,0:T(8,128)} %bitcast.17), channel_id=1, source_target_pairs={{0,12},{1,13},{2,14},{3,15},{4,8},{5,9},{6,10},{7,11},{8,4},{9,5},... | collective-permute-start | bytes 196616 | tf_op jit(solution)/shard_map/ppermute | solution.py:223
  5.0 4.9 %collective-permute-start.1 = (f32[32,512]{1,0:T(8,128)}, f32[32,512]{1,0:T(8,128)S(1)}, u32[]{:S(2)}, u32[]{:S(2)}) collective-permute-start(f32[32,512]{1,0:T(8,128)} %bitcast.18), channel_id=1, source_target_pairs={{0,4},{1,5},{2,6},{3,7},{4,0},{5,1},{6,2},{7,3},{8,12},{9,13},{10,... | collective-permute-start | bytes 196616 | tf_op jit(solution)/shard_map/ppermute | solution.py:223
  5.1 5.8 %collective-permute-start = (f32[32,512]{1,0:T(8,128)}, f32[32,512]{1,0:T(8,128)S(1)}, u32[]{:S(2)}, u32[]{:S(2)}) collective-permute-start(f32[32,512]{1,0:T(8,128)} %bitcast.19), channel_id=1, source_target_pairs={{0,8},{1,9},{2,10},{3,11},{4,12},{5,13},{6,14},{7,15},{8,0},{9,1},... | collective-permute-start | bytes 196616 | tf_op jit(solution)/shard_map/ppermute | solution.py:223
  5.6 5.3 %copy-start.1 = (f32[1,32,512]{2,1,0:T(8,128)S(1)}, f32[1,32,512]{2,1,0:T(8,128)}, u32[]{:S(2)}) copy-start(f32[1,32,512]{2,1,0:T(8,128)} %param.8) | copy-start | bytes 196612
  10.9 10.6 %collective-permute-start.8 = (f32[128,512]{1,0:T(8,128)S(1)}, f32[128,512]{1,0:T(8,128)S(1)}, u32[]{:S(2)}, u32[]{:S(2)}) collective-permute-start(f32[128,512]{1,0:T(8,128)S(1)} %pad_maximum_fusion.refs_0_), channel_id=1, source_target_pairs={{0,3},{1,2},{2,1},{3,0},{4,7},{5,6},{6,5},{7,4},{8,11},{9,10},{10,... | collective-permute-start | bytes 786440 | tf_op jit(solution)/shard_map/ppermute | solution.py:223
  13.4 12.5 %collective-permute-start.6 = (f32[128,512]{1,0:T(8,128)S(1)}, f32[128,512]{1,0:T(8,128)S(1)}, u32[]{:S(2)}, u32[]{:S(2)}) collective-permute-start(f32[128,512]{1,0:T(8,128)S(1)} %pad_maximum_fusion.refs_0_), channel_id=1, source_target_pairs={{0,1},{1,0},{2,3},{3,2},{4,5},{5,4},{6,7},{7,6},{8,9},{9,8},{10,11... | collective-permute-start | bytes 786440 | tf_op jit(solution)/shard_map/ppermute | solution.py:223
  14.0 15.8 %collective-permute-start.4 = (f32[128,512]{1,0:T(8,128)S(1)}, f32[128,512]{1,0:T(8,128)S(1)}, u32[]{:S(2)}, u32[]{:S(2)}) collective-permute-start(f32[128,512]{1,0:T(8,128)S(1)} %pad_maximum_fusion.refs_0_), channel_id=1, source_target_pairs={{0,2},{1,3},{2,0},{3,1},{4,6},{5,7},{6,4},{7,5},{8,10},{9,11},{10,... | collective-permute-start | bytes 786440 | tf_op jit(solution)/shard_map/ppermute | solution.py:223
  15.9 13.9 %copy-start = (f32[8,512]{1,0:T(8,128)S(1)}, f32[8,512]{1,0:T(8,128)}, u32[]{:S(2)}) copy-start(f32[8,512]{1,0:T(8,128)} %shard_map.73.refs_4_) | copy-start | bytes 49156
  15.9 28.8 %all-to-all-start = ((f32[16,32,512]{2,1,0:T(8,128)}), f32[16,32,512]{2,1,0:T(8,128)S(1)}, u32[]{:S(2)}, u32[]{:S(2)}) async-start(f32[16,32,512]{2,1,0:T(8,128)} %bitcast.12), calls=%async_computation | async-start | bytes 2097152 | tf_op jit(solution)/shard_map/all_to_all | solution.py:262
  21.5 9.9 %collective-permute-start.3 = (f32[128,512]{1,0:T(8,128)S(1)}, f32[128,512]{1,0:T(8,128)S(1)}, u32[]{:S(2)}, u32[]{:S(2)}) collective-permute-start(f32[128,512]{1,0:T(8,128)S(1)} %pad_maximum_fusion.refs_0_), channel_id=1, source_target_pairs={{0,16},{16,0},{1,17},{17,1},{2,18},{18,2},{3,19},{19,3},{4,20},{20... | collective-permute-start | bytes 786440 | tf_op jit(solution)/shard_map/ppermute | solution.py:230
  21.5 9.8 %collective-permute-start.9 = (f32[128,512]{1,0:T(8,128)S(1)}, f32[128,512]{1,0:T(8,128)S(1)}, u32[]{:S(2)}, u32[]{:S(2)}) collective-permute-start(f32[128,512]{1,0:T(8,128)S(1)} %collective-permute-done.8.refs_3_), channel_id=1, source_target_pairs={{0,16},{16,0},{1,17},{17,1},{2,18},{18,2},{3,19},{19,3},{4,20},{20... | collective-permute-start | bytes 786440 | tf_op jit(solution)/shard_map/ppermute | solution.py:230
  26.0 5.4 %collective-permute-start.7 = (f32[128,512]{1,0:T(8,128)S(1)}, f32[128,512]{1,0:T(8,128)S(1)}, u32[]{:S(2)}, u32[]{:S(2)}) collective-permute-start(f32[128,512]{1,0:T(8,128)S(1)} %collective-permute-done.6.refs_2_), channel_id=1, source_target_pairs={{0,16},{16,0},{1,17},{17,1},{2,18},{18,2},{3,19},{19,3},{4,20},{20... | collective-permute-start | bytes 786440 | tf_op jit(solution)/shard_map/ppermute | solution.py:230
  29.8 1.6 %collective-permute-start.5 = (f32[128,512]{1,0:T(8,128)S(1)}, f32[128,512]{1,0:T(8,128)S(1)}, u32[]{:S(2)}, u32[]{:S(2)}) collective-permute-start(f32[128,512]{1,0:T(8,128)S(1)} %collective-permute-done.4.refs_1_), channel_id=1, source_target_pairs={{0,16},{16,0},{1,17},{17,1},{2,18},{18,2},{3,19},{19,3},{4,20},{20... | collective-permute-start | bytes 786440 | tf_op jit(solution)/shard_map/ppermute | solution.py:230
  29.8 1.6 %collective-permute-start.10 = (f32[8,512]{1,0:T(8,128)S(1)}, f32[8,512]{1,0:T(8,128)S(1)}, u32[]{:S(2)}, u32[]{:S(2)}) collective-permute-start(f32[8,512]{1,0:T(8,128)S(1)} %copy-done), channel_id=1, source_target_pairs={{0,16},{16,0},{1,17},{17,1},{2,18},{18,2},{3,19},{19,3},{4,20},{20... | collective-permute-start | bytes 49160 | tf_op jit(solution)/shard_map/ppermute | solution.py:230
